TPU v7x, 256 devices: a whole 4x4x8 slice. The times are simulated.
256 devices in a mesh: dp: 8 (over y, z_hi), expert: 32 (over x, z_lo, core).
Axes of the slice: x: 4, y: 4, z: 8 (z_hi: 2, z_lo: 4; z = z_hi * 4 + z_lo), core: 2. Of those that a mesh axis runs over, the one named last changes fastest.
Arguments:
- tokens: bfloat16 [32768, 2560], P(('dp', 'expert')), may hold values from -6 to 6
- expert_ids: int32 [32768, 6], P(('dp', 'expert')), may hold values from 0 to 31, all different within a row; in each aligned block of 128 rows (0 to 127, 128 to 255, ...) at most 28 rows name the same one
- route_weight: float32 [32768, 6], P(('dp', 'expert')), may hold values from 0.03 to 0.5
- placement: int32 [32], replicated, may hold values from 0 to 31, each once
- swap_mask: int32 [1], replicated, may hold values from 1 to 15
- gate_weight: bfloat16 [32, 2560, 768], P('expert'), may hold values from -0.125 to 0.125
- up_weight: bfloat16 [32, 2560, 768], P('expert'), may hold values from -0.125 to 0.125
- down_weight: bfloat16 [32, 768, 2560], P('expert', 'dp'), may hold values from -0.21875 to 0.21875
- first_moment: bfloat16 [32, 768, 2560], P('expert', 'dp'), may hold values from -6 to 6
- second_moment: bfloat16 [32, 768, 2560], P('expert', 'dp'), may hold values from 1 to 30
- out_grad: bfloat16 [32768, 2560], P(('dp', 'expert')), may hold values from -6 to 6
Outputs:
- layer_out: bfloat16 [32768, 2560], P(('dp', 'expert'))
- new_down: bfloat16 [32, 768, 2560], P('expert', 'dp')
- new_first: bfloat16 [32, 768, 2560], P('expert', 'dp')
- new_second: bfloat16 [32, 768, 2560], P('expert', 'dp')
Inputs may be any that keep to these rules, and one draw needn't show every extreme that they name: `expert_ids`: each row names 6 different experts; among the rows of one device no expert is named more than 28 times, and in every draw some expert is named exactly 28 times by the rows of some device. `placement`: each expert appears once.
All inputs are finite; a program needn't handle non-finite values.
Results may differ from a plain program's by a relative error of at most 0.025.
Values may be sent and summed in bfloat16 or wider, within the bound.
No kernel may reach another device: no remote copies, remote signals or barrier semaphores. Data moves between devices by JAX's collectives and lax.ppermute only.
A program may use at most 128 MiB of HBM per device.

v0:
```python
import jax
import jax.numpy as jnp
from jax import lax
from jax.experimental import pallas as pl
from jax.experimental.pallas import tpu as pltpu
from jax.sharding import Mesh, PartitionSpec as P

SWAP_BITS = 4
N_Y, N_ZH, N_X, N_ZL, N_C = 4, 2, 4, 4, 2
AXES = ("y", "zh", "x", "zl", "c")
MIB = 1024 * 1024

first_decay_rate = 0.9
beta_two = 0.95
learn_rate = 0.003
adam_eps = 1e-08

G_CHUNKS = 2


def flat_index(y, z, x, c):
    z = z % 8
    return ((((y % 4) * N_ZH + z // N_ZL) * N_X + x % 4) * N_ZL + z % N_ZL) * N_C + c % 2


def permute(array, move):
    pairs = []
    for y in range(N_Y):
        for z in range(8):
            for x in range(N_X):
                for c in range(N_C):
                    pairs.append((flat_index(y, z, x, c), flat_index(*move(y, z, x, c))))
    return lax.ppermute(array, AXES, pairs)


def along(c):
    return 1 if c == 0 else -1


def z_up(array):
    return permute(array, lambda y, z, x, c: (y, z + along(c), x, c))


def z_down(array):
    return permute(array, lambda y, z, x, c: (y, z - along(c), x, c))


def z_gather(array):
    near = z_up(array)
    other = z_down(array)
    far = z_up(near)
    return array, near, other, far


def swap(array, zl=0, x=0, c=0):
    return permute(array, lambda y, z, i, j: (y, z ^ zl, i ^ x, j ^ c))


def relocate(array, jump, flip_zh=False):
    if jump == 0 and not flip_zh:
        return array

    def move(y, z, x, c):
        zl = (z % 4) ^ (jump & 3)
        zh = z // 4 ^ (1 if flip_zh else 0)
        return y, zh * 4 + zl, x ^ (jump >> 2), c

    return permute(array, move)


LIGHT = pl.CostEstimate(flops=1, bytes_accessed=1, transcendentals=0)


def params(mib, *semantics):
    return pltpu.CompilerParams(
        dimension_semantics=semantics or None, vmem_limit_bytes=mib * MIB
    )


def hold_kernel(count, start, *refs):
    out, first = refs[-1], 0
    for array in refs[:count]:
        rows = array.shape[0] - start
        out[first : first + rows, :] = array[start:, :]
        first += rows


def hold(arrays, *earlier, start=0):
    rows, width = sum(a.shape[0] - start for a in arrays), arrays[0].shape[1]
    return pl.pallas_call(
        lambda *refs: hold_kernel(len(arrays), start, *refs),
        in_specs=[pl.BlockSpec(memory_space=pltpu.VMEM) for _ in arrays]
        + [pl.BlockSpec(memory_space=pl.ANY) for _ in earlier],
        out_specs=pl.BlockSpec(memory_space=pltpu.VMEM),
        out_shape=jax.ShapeDtypeStruct((rows, width), arrays[0].dtype),
        compiler_params=params(60),
        cost_estimate=LIGHT,
        name="hold",
    )(*arrays, *earlier)


def mark_kernel(tokens, meta, out):
    width = tokens.shape[1]
    out[:, :width] = tokens[...]
    left = meta[...]
    total = None
    for turn in range(3):
        part = left.astype(jnp.bfloat16).astype(jnp.float32)
        left = left - part
        part = pltpu.roll(part, 16 * turn, 1) if turn else part
        total = part if total is None else total + part
    out[:, width:] = total.astype(jnp.bfloat16)


def mark(tokens, meta):
    rows, width = tokens.shape
    return pl.pallas_call(
        mark_kernel,
        in_specs=[pl.BlockSpec(memory_space=pltpu.VMEM)] * 2,
        out_specs=pl.BlockSpec(memory_space=pltpu.VMEM),
        out_shape=jax.ShapeDtypeStruct((rows, width + 128), jnp.bfloat16),
        compiler_params=params(60),
        cost_estimate=LIGHT,
        name="mark",
    )(tokens, meta)


def choose_kernel(wanted, other, own, *refs):
    @pl.when(wanted[0] == 1)
    def _():
        refs[-1][...] = other[...]

    @pl.when(wanted[0] != 1)
    def _():
        refs[-1][...] = own[...]


def choose(wanted, other, own, *earlier):
    return pl.pallas_call(
        choose_kernel,
        in_specs=[pl.BlockSpec(memory_space=pltpu.SMEM)]
        + [pl.BlockSpec(memory_space=pltpu.VMEM) for _ in range(2)]
        + [pl.BlockSpec(memory_space=pl.ANY) for _ in earlier],
        out_specs=pl.BlockSpec(memory_space=pltpu.VMEM),
        out_shape=jax.ShapeDtypeStruct(own.shape, own.dtype),
        compiler_params=params(60),
        cost_estimate=LIGHT,
        name="choose",
    )(wanted, other, own, *earlier)


def sum_kernel(a, b, c, d, *refs):
    total = a[...].astype(jnp.float32) + b[...].astype(jnp.float32)
    total = total + c[...].astype(jnp.float32) + d[...].astype(jnp.float32)
    refs[-1][...] = total.astype(jnp.bfloat16)


def sum_blocks(blocks, *earlier):
    return pl.pallas_call(
        sum_kernel,
        in_specs=[pl.BlockSpec(memory_space=pltpu.VMEM) for _ in blocks]
        + [pl.BlockSpec(memory_space=pl.ANY) for _ in earlier],
        out_specs=pl.BlockSpec(memory_space=pltpu.VMEM),
        out_shape=jax.ShapeDtypeStruct(blocks[0].shape, jnp.bfloat16),
        compiler_params=params(60),
        cost_estimate=LIGHT,
        name="sum",
    )(*blocks, *earlier)


def plan_kernel(cap, top, ids_here, m0, m1, m2, m3, *refs):
    slot_ref, weight_ref = refs[-2:]
    rows = m0.shape[0]
    before = lax.broadcasted_iota(jnp.int32, (rows, rows), 0)
    after = lax.broadcasted_iota(jnp.int32, (rows, rows), 1)
    earlier = (before < after).astype(jnp.float32).astype(jnp.bfloat16)
    wanted = ids_here[...]
    for s, block in enumerate((m0, m1, m2, m3)):
        meta = block[...].astype(jnp.float32).T
        scale = meta[8:16, :] + meta[24:32, :] + meta[40:48, :]
        named = jnp.zeros(wanted.shape, jnp.float32)
        weight = jnp.zeros(wanted.shape, jnp.float32)
        for k in range(top):
            same = (meta[k : k + 1, :] == wanted).astype(jnp.float32)
            named = named + same
            weight = weight + same * scale[k : k + 1, :]
        rank = jnp.dot(named.astype(jnp.bfloat16), earlier, preferred_element_type=jnp.float32)
        slot = jnp.where(named > 0.5, rank + float(s * cap), -1.0)
        slot_ref[:, s * rows : (s + 1) * rows] = slot
        weight_ref[:, s * rows : (s + 1) * rows] = weight


def make_plan(cap, top, ids_here, parts, *earlier):
    rows, width = parts[0].shape
    last = width // 128 - 1
    out = jax.ShapeDtypeStruct((ids_here.shape[0], 4 * rows), jnp.float32)
    whole = pl.BlockSpec(out.shape, lambda i: (0, 0))
    return pl.pallas_call(
        lambda *refs: plan_kernel(cap, top, *refs),
        grid=(1,),
        in_specs=[pl.BlockSpec(ids_here.shape, lambda i: (0, 0))]
        + [pl.BlockSpec((rows, 128), lambda i: (0, last)) for _ in parts]
        + [pl.BlockSpec(memory_space=pl.ANY) for _ in earlier],
        out_specs=(whole, whole),
        out_shape=(out, out),
        compiler_params=params(60, "arbitrary"),
        cost_estimate=LIGHT,
        name="plan",
    )(ids_here, *parts, *earlier)


def select_kernel(scaled, slots, weights, t0, t1, t2, t3, *refs):
    *outs, pick, scale = refs
    tokens = slots.shape[1]
    block = pick.shape[0] // 8
    base = 8 if scaled else 0

    @pl.when(pl.program_id(0) == 0)
    def _():
        place = lax.broadcasted_iota(jnp.int32, (block, tokens), 0).astype(jnp.float32)
        for d in range(8):
            hit = (slots[base + d : base + d + 1, :] == place).astype(jnp.float32)
            pick[d * block : (d + 1) * block, :] = hit.astype(jnp.bfloat16)
            if scaled:
                row = jnp.sum(hit * weights[base + d : base + d + 1, :], axis=1, keepdims=True)
                scale[d * block : (d + 1) * block, :] = jnp.broadcast_to(row, (block, 128))

    source = jnp.concatenate([t0[...], t1[...], t2[...], t3[...]], axis=0)
    rows = jnp.dot(pick[...], source, preferred_element_type=jnp.float32)
    if scaled:
        rows = (rows * scale[:, 0:1]).astype(jnp.bfloat16)
        for k, out in enumerate(outs[-4:]):
            out[...] = rows[2 * k * block : 2 * (k + 1) * block, :]
    else:
        outs[-1][...] = rows.astype(jnp.bfloat16).reshape(8, block, -1)


def select_rows(scaled, cap, plan, parts, first, width, *earlier):
    slots, weights = plan
    rows = parts[0].shape[0]
    block = 4 * cap
    tile = 256 if width % 512 else 512
    offset = first // tile
    whole = pl.BlockSpec(slots.shape, lambda j: (0, 0))
    if scaled:
        out_spec = (pl.BlockSpec((2 * block, tile), lambda j: (0, j)),) * 4
        out_shape = (jax.ShapeDtypeStruct((2 * block, width), jnp.bfloat16),) * 4
    else:
        out_spec = pl.BlockSpec((8, block, tile), lambda j: (0, 0, j))
        out_shape = jax.ShapeDtypeStruct((8, block, width), jnp.bfloat16)
    return pl.pallas_call(
        lambda *refs: select_kernel(scaled, *refs),
        grid=(width // tile,),
        in_specs=[whole, whole]
        + [pl.BlockSpec((rows, tile), lambda j: (0, j + offset)) for _ in range(4)]
        + [pl.BlockSpec(memory_space=pl.ANY) for _ in earlier],
        out_specs=out_spec,
        out_shape=out_shape,
        scratch_shapes=[
            pltpu.VMEM((8 * block, 4 * rows), jnp.bfloat16),
            pltpu.VMEM((8 * block, 128), jnp.float32),
        ],
        compiler_params=params(60, "arbitrary"),
        cost_estimate=LIGHT,
        name="select_scaled" if scaled else "select",
    )(slots, weights, *parts, *earlier)


def hidden_kernel(count, where, *refs):
    xs, (gate_w, up_w), (out, held) = refs[:count], refs[count : count + 2], refs[-2:]
    step, tile = pl.program_id(0), gate_w.shape[1]
    steps, features = held.shape[0], out.shape[1]
    gate, up, first = None, None, 0
    for x in xs:
        rows = x[...].reshape(-1, x.shape[2])
        part = slice(first, first + x.shape[2])
        first += x.shape[2]
        g = jnp.dot(rows, gate_w[part, :], preferred_element_type=jnp.float32)
        u = jnp.dot(rows, up_w[part, :], preferred_element_type=jnp.float32)
        gate, up = (g, u) if gate is None else (gate + g, up + u)
    held[step] = (gate / (1.0 + jnp.exp(-gate)) * up).astype(jnp.bfloat16)

    @pl.when(step == steps - 1)
    def _():
        shard = features // (N_Y * N_ZH)
        column = lax.broadcasted_iota(jnp.int32, (tile, features), 1)
        row = lax.broadcasted_iota(jnp.int32, (tile, features), 0)
        number = column // shard
        zh = (where[1] + number % 2) % N_ZH
        y = (where[0] + number // 2) % N_Y
        origin = (y * N_ZH + zh) * shard + (column - number * shard)
        total = None
        for s in range(steps):
            move = (row + s * tile == origin).astype(jnp.float32).astype(jnp.bfloat16)
            part = jnp.dot(held[s], move, preferred_element_type=jnp.float32)
            total = part if total is None else total + part
        out[...] = total.astype(jnp.bfloat16)


def hidden_rows(where, xs, gate_weight, up_weight, earlier):
    depth, features = gate_weight.shape
    count = xs[0].shape[0] * xs[0].shape[1]
    tile = 256
    steps = features // tile
    return pl.pallas_call(
        lambda *refs: hidden_kernel(len(xs), *refs),
        grid=(steps,),
        in_specs=[pl.BlockSpec(memory_space=pltpu.SMEM)]
        + [pl.BlockSpec(x.shape, lambda j: (0, 0, 0)) for x in xs]
        + [pl.BlockSpec((depth, tile), lambda j: (0, j)) for _ in range(2)]
        + [pl.BlockSpec(memory_space=pl.ANY) for _ in earlier],
        out_specs=pl.BlockSpec((count, features), lambda j: (0, 0)),
        out_shape=jax.ShapeDtypeStruct((count, features), jnp.bfloat16),
        scratch_shapes=[pltpu.VMEM((steps, count, tile), jnp.bfloat16)],
        compiler_params=params(60, "arbitrary"),
        name="hidden",
    )(where, *xs, gate_weight, up_weight, *earlier)


def down_kernel(hidden, d0, d1, d2, d3, out):
    weight = jnp.concatenate([d0[...], d1[...], d2[...], d3[...]], axis=0)
    rows = jnp.dot(hidden[...], weight, preferred_element_type=jnp.float32)
    out[...] = rows.astype(jnp.bfloat16).reshape(out.shape)


def down_rows(hidden, downs, cap, first, width):
    tile = 256 if width % 512 else 512
    offset = first // tile
    block = 4 * cap
    return pl.pallas_call(
        down_kernel,
        grid=(width // tile,),
        in_specs=[pl.BlockSpec(hidden.shape, lambda j: (0, 0))]
        + [pl.BlockSpec((d.shape[0], tile), lambda j: (0, j + offset)) for d in downs],
        out_specs=pl.BlockSpec((8, block, tile), lambda j: (0, 0, j)),
        out_shape=jax.ShapeDtypeStruct((8, block, width), jnp.bfloat16),
        compiler_params=params(60, "arbitrary"),
        name="down",
    )(hidden, *downs)


def grad_kernel(where, hidden, *refs):
    rows, outs, turned = refs[:5], refs[-5:-1], refs[-1]
    block = rows[0].shape[0]

    @pl.when(pl.program_id(0) == 0)
    def _():
        parts = []
        for k in range(8):
            source = (where[2] + N_X - k % 4) % N_X * 2 + (where[3] + k // 4) % 2
            parts.append(hidden[pl.ds(pl.multiple_of(source * block, 16), block), :])
        turned[...] = jnp.concatenate(parts, axis=0).T

    value = jnp.concatenate([r[...] for r in rows], axis=0)
    grad = jnp.dot(turned[...], value, preferred_element_type=jnp.float32).astype(jnp.bfloat16)
    quarter = outs[0].shape[0]
    for k, out in enumerate(outs):
        out[...] = grad[k * quarter : (k + 1) * quarter, :]


def grad_blocks(where, hidden, rows, first, width, *earlier):
    block = rows[0].shape[0] // 2
    tile = 256 if width % 512 else 512
    offset = first // tile
    quarter = hidden.shape[1] // N_Y
    spec = pl.BlockSpec((quarter, tile), lambda j: (0, j))
    out = jax.ShapeDtypeStruct((quarter, width), jnp.bfloat16)
    return pl.pallas_call(
        grad_kernel,
        grid=(width // tile,),
        in_specs=[
            pl.BlockSpec(memory_space=pltpu.SMEM),
            pl.BlockSpec(hidden.shape, lambda j: (0, 0)),
        ]
        + [pl.BlockSpec((block, tile), lambda j: (0, j + offset)) for _ in range(4)]
        + [pl.BlockSpec((4 * block, tile), lambda j: (0, j + offset))]
        + [pl.BlockSpec(memory_space=pl.ANY) for _ in earlier],
        out_specs=(spec,) * 4,
        out_shape=(out,) * 4,
        scratch_shapes=[pltpu.VMEM(hidden.shape[::-1], jnp.bfloat16)],
        compiler_params=params(60, "arbitrary"),
        name="grad",
    )(where, hidden, *rows, *earlier)


def combine_kernel(slots, weights, rows, *refs):
    *outs, high, low = refs[-6:]
    dests, block, width = rows.shape
    tokens = slots.shape[1]

    @pl.when(pl.program_id(0) == 0)
    def _():
        place = lax.broadcasted_iota(jnp.int32, (block, tokens), 0).astype(jnp.float32)
        picked = []
        for d in range(dests):
            hit = (slots[d : d + 1, :] == place).astype(jnp.float32)
            picked.append(hit * weights[d : d + 1, :])
        pick = jnp.concatenate(picked, axis=0).T
        coarse = pick.astype(jnp.bfloat16)
        high[...] = coarse
        low[...] = (pick - coarse.astype(jnp.float32)).astype(jnp.bfloat16)

    value = rows[...].reshape(-1, width)
    total = jnp.dot(high[...], value, preferred_element_type=jnp.float32)
    total = total + jnp.dot(low[...], value, preferred_element_type=jnp.float32)
    count = outs[0].shape[0]
    for s, out in enumerate(outs):
        out[...] = total[s * count : (s + 1) * count, :].astype(out.dtype)


def combine_rows(plan, rows, *earlier):
    slots, weights = plan
    width = rows.shape[2]
    tile = 256 if width % 512 else 512
    count = slots.shape[1] // 4
    whole = pl.BlockSpec((8, slots.shape[1]), lambda j: (0, 0))
    spec = pl.BlockSpec((count, tile), lambda j: (0, j))
    return pl.pallas_call(
        combine_kernel,
        grid=(width // tile,),
        in_specs=[whole, whole, pl.BlockSpec((*rows.shape[:2], tile), lambda j: (0, 0, j))]
        + [pl.BlockSpec(memory_space=pl.ANY) for _ in earlier],
        out_specs=(spec,) * 4,
        out_shape=tuple(
            jax.ShapeDtypeStruct((count, width), t)
            for t in (jnp.float32, jnp.bfloat16, jnp.bfloat16, jnp.bfloat16)
        ),
        scratch_shapes=[
            pltpu.VMEM((slots.shape[1], rows.shape[0] * rows.shape[1]), jnp.bfloat16)
            for _ in range(2)
        ],
        compiler_params=params(60, "arbitrary"),
        name="combine",
    )(slots, weights, rows, *earlier)


def plane_permute(blocks):
    out = [blocks[0]]
    for k in range(1, N_X):
        out.append(permute(blocks[k], lambda y, z, x, c, k=k: (y, z, x + k, c)))
    return out


def core_permute(blocks, *earlier):
    passed = hold(blocks, *earlier, start=blocks[0].shape[0] // 2)
    return permute(passed, lambda y, z, x, c: (y, z, x, c + 1))


def plane_exchange(rows):
    return lax.all_to_all(rows, ("x", "c"), split_axis=0, concat_axis=0, tiled=True)


def z_return(own, near, other, far):
    step = z_down(far).astype(jnp.float32) + near.astype(jnp.float32)
    from_near = z_down(step.astype(jnp.bfloat16))
    from_other = z_up(other)
    total = own + from_near.astype(jnp.float32) + from_other.astype(jnp.float32)
    return total.astype(jnp.bfloat16)


def y_move(array, k):
    return permute(array, lambda y, z, x, c: (y + k, z, x, c))


def adam(grad, weight, first, second):
    weight_old = weight.astype(jnp.float32)
    moment_one = first_decay_rate * first.astype(jnp.float32) + (1.0 - first_decay_rate) * grad
    moment_two = beta_two * second.astype(jnp.float32) + (1.0 - beta_two) * grad * grad
    updated = weight_old - learn_rate * moment_one / (jnp.sqrt(moment_two) + adam_eps)
    return tuple(v.astype(jnp.bfloat16)[None] for v in (updated, moment_one, moment_two))


def local(
    tokens,
    expert_ids,
    route_weight,
    placement,
    swap_mask,
    gate_weight,
    up_weight,
    down_weight,
    first_moment,
    second_moment,
    out_grad,
):
    tok_rows, top = expert_ids.shape
    width = tokens.shape[1]
    experts = placement.shape[0]
    cap = tok_rows * top * 7 // (6 * experts)
    jumps = range(2 ** (SWAP_BITS - 1))
    jump = jnp.clip(swap_mask[0] // 2, 0, len(jumps) - 1)
    bits = [swap_mask // 2**bit % 2 for bit in range(SWAP_BITS)]

    where = [lax.axis_index(a) for a in ("y", "zh", "x", "c")]
    where = jnp.stack(where).astype(jnp.int32)

    dest = jnp.arange(8, dtype=jnp.int32)
    ring = (where[2] + dest // 2) % N_X * 2 + (where[3] + dest) % 2
    dest = jnp.concatenate([dest, ring])
    held_at = (dest // 2) * 8 + lax.axis_index("zl") * 2 + dest % 2
    ids = jnp.arange(experts, dtype=jnp.int32)
    here = jnp.sum(jnp.where(placement[None, :] == held_at[:, None], ids[None, :], 0), axis=1)
    here = jnp.broadcast_to(here.astype(jnp.float32)[:, None], (16, tok_rows))
    numbers = jnp.pad(expert_ids.astype(jnp.float32), ((0, 0), (0, 128 - top)))
    meta = numbers + jnp.pad(route_weight, ((0, 0), (8, 120 - top)))

    x_parts = z_gather(mark(tokens, meta))
    state = hold((down_weight[0], first_moment[0], second_moment[0]))
    far_state = swap(state, x=1)
    plan = make_plan(cap, top, here, x_parts, far_state)
    x_send = select_rows(False, cap, plan, x_parts, 0, width)
    x_rows = plane_exchange(x_send)
    down = hold((down_weight[0],), x_parts[1])
    partner = permute(down, lambda y, z, x, c: (y, z + 4, x, c))
    g_parts = z_gather(hold((out_grad,), plan[0], partner))
    state = choose(bits[3], far_state, state, x_send)
    state_cores = choose(bits[0], swap(state, c=1), state, *g_parts[2:])
    state_far = swap(state_cores, zl=2)

    g_send = select_rows(True, cap, plan, g_parts, 0, width, x_rows, state_cores)
    g_rows = plane_permute(g_send)

    pair = hold((down, partner), x_send)
    downs = (pair, y_move(pair, -1), y_move(pair, -2), y_move(pair, 1))

    hidden = hidden_rows(where, [x_rows], gate_weight[0], up_weight[0], g_send[3:])
    r_send = down_rows(hidden, downs, cap, 0, width)
    returned = plane_exchange(r_send)
    state_far = choose(bits[2], state_far, state_cores, r_send)
    state = choose(bits[1], swap(state_far, zl=1), state_far)

    g_rows = (*g_rows, core_permute(g_rows, state_far))
    chunk = width // G_CHUNKS
    partials = [
        grad_blocks(where, hidden, g_rows, i * chunk, chunk, r_send) for i in range(G_CHUNKS)
    ]
    grads = []
    for i, blocks in enumerate(partials):
        moved = [blocks[0]] + [y_move(blocks[k], k) for k in (1, 2, 3)]
        earlier = (grads[-1], returned) if grads else (partials[-1][0],)
        total = sum_blocks(moved, state, *earlier)
        total = choose(bits[0], swap(total, c=1), total)
        rows = total.shape[0] // 2
        mine, theirs = lax.switch(
            jump,
            [lambda a, b, m=m: (relocate(a, m), relocate(b, m, True)) for m in jumps],
            total[:rows],
            total[rows:],
        )
        grads.append(mine.astype(jnp.float32) + theirs.astype(jnp.float32))
    new_state = adam(jnp.concatenate(grads, axis=1), *jnp.split(state, 3, axis=0))

    layer_out = z_return(*combine_rows(plan, returned, grads[0]))
    return (layer_out, *new_state)


def solution(mesh):
    fine = Mesh(mesh.devices.reshape(N_Y, N_ZH, N_X, N_ZL, N_C), AXES)
    dp, expert = ("y", "zh"), ("x", "zl", "c")
    batch, weight, state = P(dp + expert, None), P(expert, None, None), P(expert, dp, None)
    return jax.shard_map(
        local,
        mesh=fine,
        in_specs=(batch,) * 3 + (P(), P()) + (weight,) * 2 + (state,) * 3 + (batch,),
        out_specs=(batch, state, state, state),
        check_vma=False,
    )
```

profile of v0, /device:TPU:1, one launch (start us, length us, event | category | flops | bytes accessed | tf_op | source)
XLA Modules:
  0.0 342.5 jit_solution(827130336439354204)
XLA Ops:
  0.7 2.5 hold.5.own
  3.2 2.0 collective-permute-start.33
  6.2 2.0 mark.1.refs_1_.refs_2_
  8.2 5.6 %collective-permute-start.30 = (bf16[128,2688]{1,0:T(8,128)(2,1)}, bf16[128,2688]{1,0:T(8,128)(2,1)S(1)}, u32[]{:S(2)}, u32[]{:S(2)}) collective-permute-start(bf16[128,2688]{1,0:T(8,128)(2,1)} %mark.1.refs_1_.refs_2_), channel_id=1, source_target_pairs={{0,2},{1,39},{8,10},{9,47},{16,18},{17,55},{24,26},{25,63},{2,4},{... | collective-permute-start | bytes 2064392 | tf_op jit(solution)/shard_map/ppermute | solution.py:33
  13.8 14.1 %collective-permute-done.30.refs_2_.refs_3_.refs_1_ = bf16[128,2688]{1,0:T(8,128)(2,1)S(1)} collective-permute-done((bf16[128,2688]{1,0:T(8,128)(2,1)}, bf16[128,2688]{1,0:T(8,128)(2,1)S(1)}, u32[]{:S(2)}, u32[]{:S(2)}) %collective-permute-start.30) | collective-permute-done | bytes 688160 | tf_op jit(solution)/shard_map/ppermute | solution.py:33
  27.9 3.3 collective-permute-start.32
  31.5 7.6 %collective-permute-done.32.refs_4_.refs_5_ = bf16[128,2688]{1,0:T(8,128)(2,1)S(1)} collective-permute-done((bf16[128,2688]{1,0:T(8,128)(2,1)S(1)}, bf16[128,2688]{1,0:T(8,128)(2,1)S(1)}, u32[]{:S(2)}, u32[]{:S(2)}) %collective-permute-start.32) | collective-permute-done | bytes 688160 | tf_op jit(solution)/shard_map/ppermute | solution.py:33
  40.5 1.7 plan.1
  42.2 7.1 %select.94.refs_0_.refs_2_ = bf16[8,112,2560]{2,1,0:T(8,128)(2,1)} custom-call(f32[16,512]{1,0:T(8,128)} %get-tuple-element.138.refs_0_.refs_1_.slots, f32[16,512]{1,0:T(8,128)} %get-tuple-element.139.refs_1_.weights, bf16[128,2688]{1,0:T(8,128)(2,1)} %mark.1.refs_1_.refs_2_, bf16[128,2688]{1,0:T(8,128)(2,1)} %copy-done.5, bf16[128,2688]{1,0:T(8,128)(2,1)} %copy-done.8, ...), custom_call_target="tpu_custom_call" | custom-call | flops 1 | bytes 1 | tf_op jit(solution)/shard_map/select/pallas_call | solution.py:251
  49.3 7.4 %all-to-all-start = ((bf16[8,112,2560]{2,1,0:T(8,128)(2,1)}), bf16[8,112,2560]{2,1,0:T(8,128)(2,1)}, u32[]{:S(2)}, u32[]{:S(2)}) async-start(bf16[8,112,2560]{2,1,0:T(8,128)(2,1)} %select.94.refs_0_.refs_2_), calls=%async_computation | async-start | bytes 9175040 | tf_op jit(solution)/shard_map/all_to_all | solution.py:450
  56.7 1.8 hold.6.refs_0_
  58.6 4.5 %collective-permute-start.34 = (bf16[96,2560]{1,0:T(8,128)(2,1)}, bf16[96,2560]{1,0:T(8,128)(2,1)S(1)}, u32[]{:S(2)}, u32[]{:S(2)}) collective-permute-start(bf16[96,2560]{1,0:T(8,128)(2,1)} %hold.6.refs_0_), channel_id=1, source_target_pairs={{0,32},{1,33},{8,40},{9,41},{16,48},{17,49},{24,56},{25,57},{2,34}... | collective-permute-start | bytes 1474568 | tf_op jit(solution)/shard_map/ppermute | solution.py:33
  63.7 3.0 choose.6.own
  67.2 16.4 %collective-permute-done.34.refs_2_.refs_1_ = bf16[96,2560]{1,0:T(8,128)(2,1)S(1)} collective-permute-done((bf16[96,2560]{1,0:T(8,128)(2,1)}, bf16[96,2560]{1,0:T(8,128)(2,1)S(1)}, u32[]{:S(2)}, u32[]{:S(2)}) %collective-permute-start.34) | collective-permute-done | bytes 491552 | tf_op jit(solution)/shard_map/ppermute | solution.py:33
  84.4 2.0 hold.7.refs_2_
  86.4 3.2 collective-permute-start.35
  89.6 11.2 %collective-permute-done.35.refs_3_ = bf16[128,2560]{1,0:T(8,128)(2,1)S(1)} collective-permute-done((bf16[128,2560]{1,0:T(8,128)(2,1)}, bf16[128,2560]{1,0:T(8,128)(2,1)S(1)}, u32[]{:S(2)}, u32[]{:S(2)}) %collective-permute-start.35) | collective-permute-done | bytes 655392 | tf_op jit(solution)/shard_map/ppermute | solution.py:33
  100.8 3.4 collective-permute-start.37
  104.2 2.2 hold.8.d0
  106.4 2.7 collective-permute-start.39
  109.5 2.2 collective-permute-done.37.refs_1_.refs_5_
  112.6 1.2 copy-done.14
  113.8 3.0 choose.7.refs_7_.own
  117.4 6.7 %select_scaled.1 = (bf16[224,2560]{1,0:T(8,128)(2,1)}, bf16[224,2560]{1,0:T(8,128)(2,1)}, bf16[224,2560]{1,0:T(8,128)(2,1)}, bf16[224,2560]{1,0:T(8,128)(2,1)}) custom-call(f32[16,512]{1,0:T(8,128)} %get-tuple-element.138.refs_0_.refs_1_.slots, f32[16,512]{1,0:T(8,128)} %get-tuple-element.139.refs_1_.weights, bf16[128,2560]{1,0:T(8,128)(2,1)} %hold.7.refs_2_, ...), custom_call_target="tpu_custom_call" | custom-call | flops 1 | bytes 1 | tf_op jit(solution)/shard_map/select_scaled/pallas_call | solution.py:251
  124.1 1.2 collective-permute-start.42
  125.3 2.8 collective-permute-start.43
  128.1 1.9 collective-permute-start.44
  130.0 19.2 %collective-permute-start.41 = (bf16[192,2560]{1,0:T(8,128)(2,1)S(1)}, bf16[192,2560]{1,0:T(8,128)(2,1)}, u32[]{:S(2)}, u32[]{:S(2)}) collective-permute-start(bf16[192,2560]{1,0:T(8,128)(2,1)S(1)} %copy-done.7), channel_id=1, source_target_pairs={{0,64},{1,65},{8,72},{9,73},{16,80},{17,81},{24,88},{25,89},{2,66}... | collective-permute-start | bytes 2949128 | tf_op jit(solution)/shard_map/ppermute | solution.py:33
  149.8 13.2 %hidden.1 = bf16[896,768]{1,0:T(8,128)(2,1)} custom-call(s32[4]{0:T(128)} %pad_add_fusion.2.refs_0_.where, bf16[8,112,2560]{2,1,0:T(8,128)(2,1)} %all-to-all-done.refs_6_.refs_1_, bf16[2560,768]{1,0:T(8,128)(2,1)} %bitcast.20, bf16[2560,768]{1,0:T(8,128)(2,1)} %bitcast.21, bf16[224,2560]{1,0:T(8,128)(2,1)} %get-tuple-element.140.refs_4_), custom_call_target="tpu_custom_call" | custom-call | tf_op jit(solution)/shard_map/hidden/pallas_call | solution.py:305
  163.1 1.2 collective-permute-done.41.d3
  164.3 8.5 %down.1.refs_0_.refs_5_ = bf16[8,112,2560]{2,1,0:T(8,128)(2,1)} custom-call(bf16[896,768]{1,0:T(8,128)(2,1)} %hidden.1, bf16[192,2560]{1,0:T(8,128)(2,1)} %hold.8.d0, bf16[192,2560]{1,0:T(8,128)(2,1)} %collective-permute-done.39.d1, bf16[192,2560]{1,0:T(8,128)(2,1)} %collective-permute-done.40.d2, bf16[192,2560]{1,0:T(8,128)(2,1)} %collective-permute-done.41.d3), custom_call_target="tpu_custom_call" | custom-call | tf_op jit(solution)/shard_map/down/pallas_call | solution.py:330
  172.8 9.7 %collective-permute-done.45.other = bf16[288,2560]{1,0:T(8,128)(2,1)} collective-permute-done((bf16[288,2560]{1,0:T(8,128)(2,1)}, bf16[288,2560]{1,0:T(8,128)(2,1)}, u32[]{:S(2)}, u32[]{:S(2)}) %collective-permute-start.45) | collective-permute-done | bytes 1474592 | tf_op jit(solution)/shard_map/ppermute | solution.py:33
  182.5 3.0 choose.8.refs_4_.own
  187.0 3.8 %hold.9 = bf16[448,2560]{1,0:T(8,128)(2,1)} custom-call(bf16[224,2560]{1,0:T(8,128)(2,1)} %get-tuple-element.141.refs_0_, bf16[224,2560]{1,0:T(8,128)(2,1)} %copy-done.2, bf16[224,2560]{1,0:T(8,128)(2,1)} %copy-done.3, bf16[224,2560]{1,0:T(8,128)(2,1)} %collective-permute-done.44.refs_3_, bf16[288,2560]{1,0:T(8,128)(2,1)} %choose.8.refs_4_.own), custom_call_target="tpu_custom_call" | custom-call | flops 1 | bytes 1 | tf_op jit(solution)/shard_map/hold/pallas_call | solution.py:90
  190.8 1.8 collective-permute-start.46
  192.6 4.6 %all-to-all-start.1 = ((bf16[8,112,2560]{2,1,0:T(8,128)(2,1)}), bf16[8,112,2560]{2,1,0:T(8,128)(2,1)}, u32[]{:S(2)}, u32[]{:S(2)}) async-start(bf16[8,112,2560]{2,1,0:T(8,128)(2,1)} %down.1.refs_0_.refs_5_), calls=%async_computation.1 | async-start | bytes 9175040 | tf_op jit(solution)/shard_map/all_to_all | solution.py:450
  197.3 6.7 %grad.2 = (bf16[192,1280]{1,0:T(8,128)(2,1)}, bf16[192,1280]{1,0:T(8,128)(2,1)}, bf16[192,1280]{1,0:T(8,128)(2,1)}, bf16[192,1280]{1,0:T(8,128)(2,1)}) custom-call(s32[4]{0:T(128)} %pad_add_fusion.2.refs_0_.where, bf16[896,768]{1,0:T(8,128)(2,1)} %hidden.1, bf16[224,2560]{1,0:T(8,128)(2,1)} %get-tuple-element.141.refs_0_, bf16[224,2560]{1,0:T(8,128)(2,1)} %copy-done.2, ...), custom_call_target="tpu_custom_call" | custom-call | tf_op jit(solution)/shard_map/grad/pallas_call | solution.py:368
  204.0 1.3 collective-permute-start.47
  205.4 2.6 collective-permute-start.48
  209.1 22.0 %collective-permute-done.50.other = bf16[288,2560]{1,0:T(8,128)(2,1)S(1)} collective-permute-done((bf16[288,2560]{1,0:T(8,128)(2,1)S(1)}, bf16[288,2560]{1,0:T(8,128)(2,1)S(1)}, u32[]{:S(2)}, u32[]{:S(2)}) %collective-permute-start.50) | collective-permute-done | bytes 1474592 | tf_op jit(solution)/shard_map/ppermute | solution.py:33
  231.1 1.1 copy-done.13
  232.2 3.0 choose.9.refs_0_
  235.3 6.8 %grad.3 = (bf16[192,1280]{1,0:T(8,128)(2,1)}, bf16[192,1280]{1,0:T(8,128)(2,1)}, bf16[192,1280]{1,0:T(8,128)(2,1)}, bf16[192,1280]{1,0:T(8,128)(2,1)}) custom-call(s32[4]{0:T(128)} %pad_add_fusion.2.refs_0_.where, bf16[896,768]{1,0:T(8,128)(2,1)} %hidden.1, bf16[224,2560]{1,0:T(8,128)(2,1)} %get-tuple-element.141.refs_0_, bf16[224,2560]{1,0:T(8,128)(2,1)} %copy-done.2, ...), custom_call_target="tpu_custom_call" | custom-call | tf_op jit(solution)/shard_map/grad/pallas_call | solution.py:368
  243.0 2.5 sum.2.own
  246.4 1.3 collective-permute-start.55
  247.7 11.2 %collective-permute-start.56 = (bf16[192,1280]{1,0:T(8,128)(2,1)}, bf16[192,1280]{1,0:T(8,128)(2,1)S(1)}, u32[]{:S(2)}, u32[]{:S(2)}) collective-permute-start(bf16[192,1280]{1,0:T(8,128)(2,1)} %get-tuple-element.156), channel_id=1, source_target_pairs={{0,128},{1,129},{8,136},{9,137},{16,144},{17,145},{24,152},{25,153... | collective-permute-start | bytes 1474568 | tf_op jit(solution)/shard_map/ppermute | solution.py:33
  260.8 2.0 choose.10
  263.9 14.9 %conditional.8 = (bf16[96,1280]{1,0:T(8,128)(2,1)S(1)}, bf16[96,1280]{1,0:T(8,128)(2,1)}) conditional(s32[]{:T(128)} %clamp.4, (bf16[96,1280]{1,0:T(8,128)(2,1)S(1)}, bf16[96,1280]{1,0:T(8,128)(2,1)S(1)}) %tuple.140, (bf16[96,1280]{1,0:T(8,128)(2,1)S(1)}, bf16[96,1280]{1,0:T(8,128)(2,1)S(1)}) %fusion.9, ...), branch_computations={%region_1.2_spmd, %region_2.3_spmd, %region_3.4_spmd, %region_4.5_... | conditional | bytes 2457696
  263.9 1.4 collective-permute-start.7
  265.3 5.1 %collective-permute-start.8 = (bf16[96,1280]{1,0:T(8,128)(2,1)S(1)}, bf16[96,1280]{1,0:T(8,128)(2,1)}, u32[]{:S(2)}, u32[]{:S(2)}) collective-permute-start(bf16[96,1280]{1,0:T(8,128)(2,1)S(1)} %get-tuple-element.89), channel_id=1, source_target_pairs={{0,40},{1,41},{8,32},{9,33},{16,56},{17,57},{24,48},{25,49},{2,42}... | collective-permute-start | bytes 737288 | tf_op jit(solution)/shard_map/cond/branch_4_fun/ppermute | solution.py:33
  270.6 8.1 %collective-permute-done.8 = bf16[96,1280]{1,0:T(8,128)(2,1)} collective-permute-done((bf16[96,1280]{1,0:T(8,128)(2,1)S(1)}, bf16[96,1280]{1,0:T(8,128)(2,1)}, u32[]{:S(2)}, u32[]{:S(2)}) %collective-permute-start.8) | collective-permute-done | bytes 245792 | tf_op jit(solution)/shard_map/cond/branch_4_fun/ppermute | solution.py:33
  278.8 1.8 convert_add_fusion.1.refs_0_.refs_1_
  281.6 2.5 sum.3.own
  284.1 2.2 collective-permute-start.58
  286.4 9.0 %combine.1 = (f32[128,2560]{1,0:T(8,128)}, bf16[128,2560]{1,0:T(8,128)(2,1)}, bf16[128,2560]{1,0:T(8,128)(2,1)}, bf16[128,2560]{1,0:T(8,128)(2,1)}) custom-call(f32[16,512]{1,0:T(8,128)} %get-tuple-element.138.refs_0_.refs_1_.slots, f32[16,512]{1,0:T(8,128)} %get-tuple-element.139.refs_1_.weights, bf16[8,112,2560]{2,1,0:T(8,128)(2,1)} %all-to-all-done.1.rows.refs_2_, ...), custom_call_target="tpu_custom_call" | custom-call | tf_op jit(solution)/shard_map/combine/pallas_call | solution.py:418
  295.3 3.2 collective-permute-start.52
  299.5 2.0 choose.11
  302.6 26.6 %conditional.9 = (bf16[96,1280]{1,0:T(8,128)(2,1)S(1)}, bf16[96,1280]{1,0:T(8,128)(2,1)}) conditional(s32[]{:T(128)} %clamp.4, (bf16[96,1280]{1,0:T(8,128)(2,1)S(1)}, bf16[96,1280]{1,0:T(8,128)(2,1)S(1)}) %tuple.142, (bf16[96,1280]{1,0:T(8,128)(2,1)S(1)}, bf16[96,1280]{1,0:T(8,128)(2,1)S(1)}) %fusion.8, ...), branch_computations={%region_9.10_spmd, %region_10.11_spmd, %region_11.12_spmd, %region... | conditional | bytes 2457696
  302.9 5.9 %collective-permute-start.23 = (bf16[96,1280]{1,0:T(8,128)(2,1)S(1)}, bf16[96,1280]{1,0:T(8,128)(2,1)}, u32[]{:S(2)}, u32[]{:S(2)}) collective-permute-start(bf16[96,1280]{1,0:T(8,128)(2,1)S(1)} %get-tuple-element.105), channel_id=1, source_target_pairs={{0,40},{1,41},{8,32},{9,33},{16,56},{17,57},{24,48},{25,49},{2,42}... | collective-permute-start | bytes 737288 | tf_op jit(solution)/shard_map/cond/branch_4_fun/ppermute | solution.py:33
  308.9 1.2 collective-permute-done.22
  310.1 19.1 %collective-permute-done.23 = bf16[96,1280]{1,0:T(8,128)(2,1)} collective-permute-done((bf16[96,1280]{1,0:T(8,128)(2,1)S(1)}, bf16[96,1280]{1,0:T(8,128)(2,1)}, u32[]{:S(2)}, u32[]{:S(2)}) %collective-permute-start.23) | collective-permute-done | bytes 245792 | tf_op jit(solution)/shard_map/cond/branch_4_fun/ppermute | solution.py:33
  329.2 1.1 convert_add_fusion
  330.8 1.7 convert_bitcast_fusion
  332.5 8.8 %collective-permute-done.53 = bf16[128,2560]{1,0:T(8,128)(2,1)S(1)} collective-permute-done((bf16[128,2560]{1,0:T(8,128)(2,1)S(1)}, bf16[128,2560]{1,0:T(8,128)(2,1)S(1)}, u32[]{:S(2)}, u32[]{:S(2)}) %collective-permute-start.53) | collective-permute-done | bytes 655392 | tf_op jit(solution)/shard_map/ppermute | solution.py:33
  (108 shorter events, 18.8 us)
Async XLA Ops:
  0.6 4.6 %copy-start.26 = (s32[128,6]{0,1:T(8,128)S(1)}, s32[128,6]{0,1:T(8,128)}, u32[]{:S(2)}) copy-start(s32[128,6]{0,1:T(8,128)} %param.28) | copy-start | bytes 9220
  0.6 4.7 %copy-start.25 = (f32[128,6]{0,1:T(8,128)S(1)}, f32[128,6]{0,1:T(8,128)}, u32[]{:S(2)}) copy-start(f32[128,6]{0,1:T(8,128)} %param.29) | copy-start | bytes 9220
  3.2 28.1 %copy-start.28 = (s32[32]{0:T(128)S(1)}, s32[32]{0:T(128)}, u32[]{:S(2)}) copy-start(s32[32]{0:T(128)} %param.30) | copy-start | bytes 388
  3.2 35.9 %collective-permute-start.33 = (bf16[288,2560]{1,0:T(8,128)(2,1)}, bf16[288,2560]{1,0:T(8,128)(2,1)S(1)}, u32[]{:S(2)}, u32[]{:S(2)}) collective-permute-start(bf16[288,2560]{1,0:T(8,128)(2,1)} %hold.5.own), channel_id=1, source_target_pairs={{0,8},{1,9},{8,0},{9,1},{16,24},{17,25},{24,16},{25,17},{2,10},{3,... | collective-permute-start | bytes 4423688 | tf_op jit(solution)/shard_map/ppermute | solution.py:33
  8.2 19.7 %collective-permute-start.30 = (bf16[128,2688]{1,0:T(8,128)(2,1)}, bf16[128,2688]{1,0:T(8,128)(2,1)S(1)}, u32[]{:S(2)}, u32[]{:S(2)}) collective-permute-start(bf16[128,2688]{1,0:T(8,128)(2,1)} %mark.1.refs_1_.refs_2_), channel_id=1, source_target_pairs={{0,2},{1,39},{8,10},{9,47},{16,18},{17,55},{24,26},{25,63},{2,4},{... | collective-permute-start | bytes 2064392 | tf_op jit(solution)/shard_map/ppermute | solution.py:33
  13.8 17.7 %collective-permute-start.31 = (bf16[128,2688]{1,0:T(8,128)(2,1)}, bf16[128,2688]{1,0:T(8,128)(2,1)S(1)}, u32[]{:S(2)}, u32[]{:S(2)}) collective-permute-start(bf16[128,2688]{1,0:T(8,128)(2,1)} %mark.1.refs_1_.refs_2_), channel_id=1, source_target_pairs={{0,38},{1,3},{8,46},{9,11},{16,54},{17,19},{24,62},{25,27},{2,0},{... | collective-permute-start | bytes 2064392 | tf_op jit(solution)/shard_map/ppermute | solution.py:33
  27.9 12.0 %copy-start.5 = (bf16[128,2688]{1,0:T(8,128)(2,1)}, bf16[128,2688]{1,0:T(8,128)(2,1)S(1)}, u32[]{:S(2)}) copy-start(bf16[128,2688]{1,0:T(8,128)(2,1)S(1)} %collective-permute-done.30.refs_2_.refs_3_.refs_1_) | copy-start | bytes 2064388
  27.9 11.2 %collective-permute-start.32 = (bf16[128,2688]{1,0:T(8,128)(2,1)S(1)}, bf16[128,2688]{1,0:T(8,128)(2,1)S(1)}, u32[]{:S(2)}, u32[]{:S(2)}) collective-permute-start(bf16[128,2688]{1,0:T(8,128)(2,1)S(1)} %collective-permute-done.30.refs_2_.refs_3_.refs_1_), channel_id=1, source_target_pairs={{0,2},{1,39},{8,10},{9,47},{16,18},{17,55},{24,26},{25,63},{2,4},{... | collective-permute-start | bytes 2064392 | tf_op jit(solution)/shard_map/ppermute | solution.py:33
  31.5 8.4 %copy-start.8 = (bf16[128,2688]{1,0:T(8,128)(2,1)}, bf16[128,2688]{1,0:T(8,128)(2,1)S(1)}, u32[]{:S(2)}) copy-start(bf16[128,2688]{1,0:T(8,128)(2,1)S(1)} %collective-permute-done.31.refs_3_.refs_4_) | copy-start | bytes 2064388
  39.1 0.9 copy-start.9
  39.1 1.4 copy-start.6
  49.3 68.2 %all-to-all-start = ((bf16[8,112,2560]{2,1,0:T(8,128)(2,1)}), bf16[8,112,2560]{2,1,0:T(8,128)(2,1)}, u32[]{:S(2)}, u32[]{:S(2)}) async-start(bf16[8,112,2560]{2,1,0:T(8,128)(2,1)} %select.94.refs_0_.refs_2_), calls=%async_computation | async-start | bytes 9175040 | tf_op jit(solution)/shard_map/all_to_all | solution.py:450
  58.6 25.1 %collective-permute-start.34 = (bf16[96,2560]{1,0:T(8,128)(2,1)}, bf16[96,2560]{1,0:T(8,128)(2,1)S(1)}, u32[]{:S(2)}, u32[]{:S(2)}) collective-permute-start(bf16[96,2560]{1,0:T(8,128)(2,1)} %hold.6.refs_0_), channel_id=1, source_target_pairs={{0,32},{1,33},{8,40},{9,41},{16,48},{17,49},{24,56},{25,57},{2,34}... | collective-permute-start | bytes 1474568 | tf_op jit(solution)/shard_map/ppermute | solution.py:33
  66.8 45.0 %collective-permute-start.38 = (bf16[288,2560]{1,0:T(8,128)(2,1)}, bf16[288,2560]{1,0:T(8,128)(2,1)S(1)}, u32[]{:S(2)}, u32[]{:S(2)}) collective-permute-start(bf16[288,2560]{1,0:T(8,128)(2,1)} %choose.6.own), channel_id=1, source_target_pairs={{0,1},{1,0},{8,9},{9,8},{16,17},{17,16},{24,25},{25,24},{2,3},{3,2... | collective-permute-start | bytes 4423688 | tf_op jit(solution)/shard_map/ppermute | solution.py:33
  83.6 0.8 copy-start.12
  86.4 14.4 %collective-permute-start.35 = (bf16[128,2560]{1,0:T(8,128)(2,1)}, bf16[128,2560]{1,0:T(8,128)(2,1)S(1)}, u32[]{:S(2)}, u32[]{:S(2)}) collective-permute-start(bf16[128,2560]{1,0:T(8,128)(2,1)} %hold.7.refs_2_), channel_id=1, source_target_pairs={{0,2},{1,39},{8,10},{9,47},{16,18},{17,55},{24,26},{25,63},{2,4},{... | collective-permute-start | bytes 1966088 | tf_op jit(solution)/shard_map/ppermute | solution.py:33
  89.6 19.9 %collective-permute-start.36 = (bf16[128,2560]{1,0:T(8,128)(2,1)}, bf16[128,2560]{1,0:T(8,128)(2,1)S(1)}, u32[]{:S(2)}, u32[]{:S(2)}) collective-permute-start(bf16[128,2560]{1,0:T(8,128)(2,1)} %hold.7.refs_2_), channel_id=1, source_target_pairs={{0,38},{1,3},{8,46},{9,11},{16,54},{17,19},{24,62},{25,27},{2,0},{... | collective-permute-start | bytes 1966088 | tf_op jit(solution)/shard_map/ppermute | solution.py:33
  100.8 5.6 %copy-start.16 = (bf16[128,2560]{1,0:T(8,128)(2,1)}, bf16[128,2560]{1,0:T(8,128)(2,1)S(1)}, u32[]{:S(2)}) copy-start(bf16[128,2560]{1,0:T(8,128)(2,1)S(1)} %collective-permute-done.35.refs_3_) | copy-start | bytes 1966084
  100.8 10.9 %collective-permute-start.37 = (bf16[128,2560]{1,0:T(8,128)(2,1)S(1)}, bf16[128,2560]{1,0:T(8,128)(2,1)S(1)}, u32[]{:S(2)}, u32[]{:S(2)}) collective-permute-start(bf16[128,2560]{1,0:T(8,128)(2,1)S(1)} %collective-permute-done.35.refs_3_), channel_id=1, source_target_pairs={{0,2},{1,39},{8,10},{9,47},{16,18},{17,55},{24,26},{25,63},{2,4},{... | collective-permute-start | bytes 1966088 | tf_op jit(solution)/shard_map/ppermute | solution.py:33
  106.4 21.7 %collective-permute-start.39 = (bf16[192,2560]{1,0:T(8,128)(2,1)}, bf16[192,2560]{1,0:T(8,128)(2,1)}, u32[]{:S(2)}, u32[]{:S(2)}) collective-permute-start(bf16[192,2560]{1,0:T(8,128)(2,1)} %hold.8.d0), channel_id=1, source_target_pairs={{0,192},{1,193},{8,200},{9,201},{16,208},{17,209},{24,216},{25,217... | collective-permute-start | bytes 2949128 | tf_op jit(solution)/shard_map/ppermute | solution.py:33
  109.2 20.8 %collective-permute-start.40 = (bf16[192,2560]{1,0:T(8,128)(2,1)}, bf16[192,2560]{1,0:T(8,128)(2,1)}, u32[]{:S(2)}, u32[]{:S(2)}) collective-permute-start(bf16[192,2560]{1,0:T(8,128)(2,1)} %hold.8.d0), channel_id=1, source_target_pairs={{0,128},{1,129},{8,136},{9,137},{16,144},{17,145},{24,152},{25,153... | collective-permute-start | bytes 2949128 | tf_op jit(solution)/shard_map/ppermute | solution.py:33
  109.5 2.2 copy-start.10
  111.8 0.9 copy-start.11
  112.6 1.2 copy-start.14
  116.8 13.1 %copy-start.7 = (bf16[192,2560]{1,0:T(8,128)(2,1)S(1)}, bf16[192,2560]{1,0:T(8,128)(2,1)}, u32[]{:S(2)}) copy-start(bf16[192,2560]{1,0:T(8,128)(2,1)} %hold.8.d0) | copy-start | bytes 2949124
  116.8 65.7 %collective-permute-start.45 = (bf16[288,2560]{1,0:T(8,128)(2,1)}, bf16[288,2560]{1,0:T(8,128)(2,1)}, u32[]{:S(2)}, u32[]{:S(2)}) collective-permute-start(bf16[288,2560]{1,0:T(8,128)(2,1)} %choose.7.refs_7_.own), channel_id=1, source_target_pairs={{0,4},{1,5},{8,12},{9,13},{16,20},{17,21},{24,28},{25,29},{2,6},{3... | collective-permute-start | bytes 4423688 | tf_op jit(solution)/shard_map/ppermute | solution.py:33
  124.1 61.4 %collective-permute-start.42 = (bf16[224,2560]{1,0:T(8,128)(2,1)}, bf16[224,2560]{1,0:T(8,128)(2,1)S(1)}, u32[]{:S(2)}, u32[]{:S(2)}) collective-permute-start(bf16[224,2560]{1,0:T(8,128)(2,1)} %get-tuple-element.142), channel_id=1, source_target_pairs={{0,8},{1,9},{8,16},{9,17},{16,24},{17,25},{24,0},{25,1},{2,10},{3,... | collective-permute-start | bytes 3440648 | tf_op jit(solution)/shard_map/ppermute | solution.py:33
  125.3 60.2 %collective-permute-start.43 = (bf16[224,2560]{1,0:T(8,128)(2,1)}, bf16[224,2560]{1,0:T(8,128)(2,1)S(1)}, u32[]{:S(2)}, u32[]{:S(2)}) collective-permute-start(bf16[224,2560]{1,0:T(8,128)(2,1)} %get-tuple-element.143), channel_id=1, source_target_pairs={{0,16},{1,17},{8,24},{9,25},{16,0},{17,1},{24,8},{25,9},{2,18},{3,... | collective-permute-start | bytes 3440648 | tf_op jit(solution)/shard_map/ppermute | solution.py:33
  128.1 57.5 %collective-permute-start.44 = (bf16[224,2560]{1,0:T(8,128)(2,1)}, bf16[224,2560]{1,0:T(8,128)(2,1)}, u32[]{:S(2)}, u32[]{:S(2)}) collective-permute-start(bf16[224,2560]{1,0:T(8,128)(2,1)} %get-tuple-element.140.refs_4_), channel_id=1, source_target_pairs={{0,24},{1,25},{8,0},{9,1},{16,8},{17,9},{24,16},{25,17},{2,26},{3,... | collective-permute-start | bytes 3440648 | tf_op jit(solution)/shard_map/ppermute | solution.py:33
  130.0 34.3 %collective-permute-start.41 = (bf16[192,2560]{1,0:T(8,128)(2,1)S(1)}, bf16[192,2560]{1,0:T(8,128)(2,1)}, u32[]{:S(2)}, u32[]{:S(2)}) collective-permute-start(bf16[192,2560]{1,0:T(8,128)(2,1)S(1)} %copy-done.7), channel_id=1, source_target_pairs={{0,64},{1,65},{8,72},{9,73},{16,80},{17,81},{24,88},{25,89},{2,66}... | collective-permute-start | bytes 2949128 | tf_op jit(solution)/shard_map/ppermute | solution.py:33
  185.6 1.0 copy-start.2
  185.6 1.4 copy-start.3
  190.8 6.5 %copy-start.1 = (bf16[288,2560]{1,0:T(8,128)(2,1)S(1)}, bf16[288,2560]{1,0:T(8,128)(2,1)}, u32[]{:S(2)}) copy-start(bf16[288,2560]{1,0:T(8,128)(2,1)} %choose.8.refs_4_.own) | copy-start | bytes 4423684
  190.8 6.5 %collective-permute-start.46 = (bf16[448,2560]{1,0:T(8,128)(2,1)}, bf16[448,2560]{1,0:T(8,128)(2,1)}, u32[]{:S(2)}, u32[]{:S(2)}) collective-permute-start(bf16[448,2560]{1,0:T(8,128)(2,1)} %hold.9), channel_id=1, source_target_pairs={{0,1},{1,0},{8,9},{9,8},{16,17},{17,16},{24,25},{25,24},{2,3},{3,2... | collective-permute-start | bytes 6881288 | tf_op jit(solution)/shard_map/ppermute | solution.py:33
  192.6 88.0 %all-to-all-start.1 = ((bf16[8,112,2560]{2,1,0:T(8,128)(2,1)}), bf16[8,112,2560]{2,1,0:T(8,128)(2,1)}, u32[]{:S(2)}, u32[]{:S(2)}) async-start(bf16[8,112,2560]{2,1,0:T(8,128)(2,1)} %down.1.refs_0_.refs_5_), calls=%async_computation.1 | async-start | bytes 9175040 | tf_op jit(solution)/shard_map/all_to_all | solution.py:450
  197.2 33.9 %collective-permute-start.50 = (bf16[288,2560]{1,0:T(8,128)(2,1)S(1)}, bf16[288,2560]{1,0:T(8,128)(2,1)S(1)}, u32[]{:S(2)}, u32[]{:S(2)}) collective-permute-start(bf16[288,2560]{1,0:T(8,128)(2,1)S(1)} %copy-done.1), channel_id=1, source_target_pairs={{0,2},{1,3},{8,10},{9,11},{16,18},{17,19},{24,26},{25,27},{2,0},{3... | collective-permute-start | bytes 4423688 | tf_op jit(solution)/shard_map/ppermute | solution.py:33
  204.0 38.0 %collective-permute-start.47 = (bf16[192,1280]{1,0:T(8,128)(2,1)}, bf16[192,1280]{1,0:T(8,128)(2,1)S(1)}, u32[]{:S(2)}, u32[]{:S(2)}) collective-permute-start(bf16[192,1280]{1,0:T(8,128)(2,1)} %get-tuple-element.145), channel_id=1, source_target_pairs={{0,64},{1,65},{8,72},{9,73},{16,80},{17,81},{24,88},{25,89},{2,66}... | collective-permute-start | bytes 1474568 | tf_op jit(solution)/shard_map/ppermute | solution.py:33
  205.4 36.7 %collective-permute-start.48 = (bf16[192,1280]{1,0:T(8,128)(2,1)}, bf16[192,1280]{1,0:T(8,128)(2,1)S(1)}, u32[]{:S(2)}, u32[]{:S(2)}) collective-permute-start(bf16[192,1280]{1,0:T(8,128)(2,1)} %get-tuple-element.146), channel_id=1, source_target_pairs={{0,128},{1,129},{8,136},{9,137},{16,144},{17,145},{24,152},{25,153... | collective-permute-start | bytes 1474568 | tf_op jit(solution)/shard_map/ppermute | solution.py:33
  208.0 34.1 %collective-permute-start.49 = (bf16[192,1280]{1,0:T(8,128)(2,1)}, bf16[192,1280]{1,0:T(8,128)(2,1)}, u32[]{:S(2)}, u32[]{:S(2)}) collective-permute-start(bf16[192,1280]{1,0:T(8,128)(2,1)} %get-tuple-element.147), channel_id=1, source_target_pairs={{0,192},{1,193},{8,200},{9,201},{16,208},{17,209},{24,216},{25,217... | collective-permute-start | bytes 1474568 | tf_op jit(solution)/shard_map/ppermute | solution.py:33
  231.1 1.1 copy-start.13
  242.0 0.8 copy-start.21
  242.1 0.9 copy-start.22
  243.0 15.9 %copy-start.27 = (bf16[192,1280]{1,0:T(8,128)(2,1)S(1)}, bf16[192,1280]{1,0:T(8,128)(2,1)}, u32[]{:S(2)}) copy-start(bf16[192,1280]{1,0:T(8,128)(2,1)} %get-tuple-element.157) | copy-start | bytes 1474564
  245.5 14.5 %collective-permute-start.51 = (bf16[192,1280]{1,0:T(8,128)(2,1)}, bf16[192,1280]{1,0:T(8,128)(2,1)S(1)}, u32[]{:S(2)}, u32[]{:S(2)}) collective-permute-start(bf16[192,1280]{1,0:T(8,128)(2,1)} %sum.2.own), channel_id=1, source_target_pairs={{0,1},{1,0},{8,9},{9,8},{16,17},{17,16},{24,25},{25,24},{2,3},{3,2... | collective-permute-start | bytes 1474568 | tf_op jit(solution)/shard_map/ppermute | solution.py:33
  246.4 34.1 %collective-permute-start.55 = (bf16[192,1280]{1,0:T(8,128)(2,1)}, bf16[192,1280]{1,0:T(8,128)(2,1)S(1)}, u32[]{:S(2)}, u32[]{:S(2)}) collective-permute-start(bf16[192,1280]{1,0:T(8,128)(2,1)} %get-tuple-element.155), channel_id=1, source_target_pairs={{0,64},{1,65},{8,72},{9,73},{16,80},{17,81},{24,88},{25,89},{2,66}... | collective-permute-start | bytes 1474568 | tf_op jit(solution)/shard_map/ppermute | solution.py:33
  247.7 32.9 %collective-permute-start.56 = (bf16[192,1280]{1,0:T(8,128)(2,1)}, bf16[192,1280]{1,0:T(8,128)(2,1)S(1)}, u32[]{:S(2)}, u32[]{:S(2)}) collective-permute-start(bf16[192,1280]{1,0:T(8,128)(2,1)} %get-tuple-element.156), channel_id=1, source_target_pairs={{0,128},{1,129},{8,136},{9,137},{16,144},{17,145},{24,152},{25,153... | collective-permute-start | bytes 1474568 | tf_op jit(solution)/shard_map/ppermute | solution.py:33
  258.9 21.6 %collective-permute-start.57 = (bf16[192,1280]{1,0:T(8,128)(2,1)S(1)}, bf16[192,1280]{1,0:T(8,128)(2,1)S(1)}, u32[]{:S(2)}, u32[]{:S(2)}) collective-permute-start(bf16[192,1280]{1,0:T(8,128)(2,1)S(1)} %copy-done.27), channel_id=1, source_target_pairs={{0,192},{1,193},{8,200},{9,201},{16,208},{17,209},{24,216},{25,217... | collective-permute-start | bytes 1474568 | tf_op jit(solution)/shard_map/ppermute | solution.py:33
  260.0 0.8 copy-start.23
  263.9 6.7 %collective-permute-start.7 = (bf16[96,1280]{1,0:T(8,128)(2,1)S(1)}, bf16[96,1280]{1,0:T(8,128)(2,1)S(1)}, u32[]{:S(2)}, u32[]{:S(2)}) collective-permute-start(bf16[96,1280]{1,0:T(8,128)(2,1)S(1)} %get-tuple-element.88), channel_id=1, source_target_pairs={{0,8},{1,9},{8,0},{9,1},{16,24},{17,25},{24,16},{25,17},{2,10},{3,... | collective-permute-start | bytes 737288 | tf_op jit(solution)/shard_map/cond/branch_4_fun/ppermute | solution.py:33
  265.3 13.4 %collective-permute-start.8 = (bf16[96,1280]{1,0:T(8,128)(2,1)S(1)}, bf16[96,1280]{1,0:T(8,128)(2,1)}, u32[]{:S(2)}, u32[]{:S(2)}) collective-permute-start(bf16[96,1280]{1,0:T(8,128)(2,1)S(1)} %get-tuple-element.89), channel_id=1, source_target_pairs={{0,40},{1,41},{8,32},{9,33},{16,56},{17,57},{24,48},{25,49},{2,42}... | collective-permute-start | bytes 737288 | tf_op jit(solution)/shard_map/cond/branch_4_fun/ppermute | solution.py:33
  280.5 0.8 copy-start.18
  280.5 0.9 copy-start.19
  280.6 1.1 copy-start.20
  284.1 14.6 %collective-permute-start.58 = (bf16[192,1280]{1,0:T(8,128)(2,1)}, bf16[192,1280]{1,0:T(8,128)(2,1)S(1)}, u32[]{:S(2)}, u32[]{:S(2)}) collective-permute-start(bf16[192,1280]{1,0:T(8,128)(2,1)} %sum.3.own), channel_id=1, source_target_pairs={{0,1},{1,0},{8,9},{9,8},{16,17},{17,16},{24,25},{25,24},{2,3},{3,2... | collective-permute-start | bytes 1474568 | tf_op jit(solution)/shard_map/ppermute | solution.py:33
  295.3 35.0 %collective-permute-start.52 = (bf16[128,2560]{1,0:T(8,128)(2,1)}, bf16[128,2560]{1,0:T(8,128)(2,1)S(1)}, u32[]{:S(2)}, u32[]{:S(2)}) collective-permute-start(bf16[128,2560]{1,0:T(8,128)(2,1)} %get-tuple-element.152), channel_id=1, source_target_pairs={{0,38},{1,3},{8,46},{9,11},{16,54},{17,19},{24,62},{25,27},{2,0},{... | collective-permute-start | bytes 1966088 | tf_op jit(solution)/shard_map/ppermute | solution.py:33
  298.5 33.9 %collective-permute-start.54 = (bf16[128,2560]{1,0:T(8,128)(2,1)}, bf16[128,2560]{1,0:T(8,128)(2,1)S(1)}, u32[]{:S(2)}, u32[]{:S(2)}) collective-permute-start(bf16[128,2560]{1,0:T(8,128)(2,1)} %get-tuple-element.154), channel_id=1, source_target_pairs={{0,2},{1,39},{8,10},{9,47},{16,18},{17,55},{24,26},{25,63},{2,4},{... | collective-permute-start | bytes 1966088 | tf_op jit(solution)/shard_map/ppermute | solution.py:33
  298.7 0.8 copy-start.24
  302.6 27.7 %copy-start.17 = (bf16[128,2560]{1,0:T(8,128)(2,1)S(1)}, bf16[128,2560]{1,0:T(8,128)(2,1)}, u32[]{:S(2)}) copy-start(bf16[128,2560]{1,0:T(8,128)(2,1)} %get-tuple-element.153) | copy-start | bytes 1966084
  302.6 7.4 %collective-permute-start.22 = (bf16[96,1280]{1,0:T(8,128)(2,1)S(1)}, bf16[96,1280]{1,0:T(8,128)(2,1)S(1)}, u32[]{:S(2)}, u32[]{:S(2)}) collective-permute-start(bf16[96,1280]{1,0:T(8,128)(2,1)S(1)} %get-tuple-element.104), channel_id=1, source_target_pairs={{0,8},{1,9},{8,0},{9,1},{16,24},{17,25},{24,16},{25,17},{2,10},{3,... | collective-permute-start | bytes 737288 | tf_op jit(solution)/shard_map/cond/branch_4_fun/ppermute | solution.py:33
  302.9 26.2 %collective-permute-start.23 = (bf16[96,1280]{1,0:T(8,128)(2,1)S(1)}, bf16[96,1280]{1,0:T(8,128)(2,1)}, u32[]{:S(2)}, u32[]{:S(2)}) collective-permute-start(bf16[96,1280]{1,0:T(8,128)(2,1)S(1)} %get-tuple-element.105), channel_id=1, source_target_pairs={{0,40},{1,41},{8,32},{9,33},{16,56},{17,57},{24,48},{25,49},{2,42}... | collective-permute-start | bytes 737288 | tf_op jit(solution)/shard_map/cond/branch_4_fun/ppermute | solution.py:33
  329.2 1.5 copy-start
  329.2 1.6 copy-start.4
  330.5 10.7 %copy-start.15 = (f32[128,2560]{1,0:T(8,128)S(1)}, f32[128,2560]{1,0:T(8,128)}, u32[]{:S(2)}) copy-start(f32[128,2560]{1,0:T(8,128)} %get-tuple-element.151) | copy-start | bytes 3932164
  330.5 10.7 %collective-permute-start.53 = (bf16[128,2560]{1,0:T(8,128)(2,1)S(1)}, bf16[128,2560]{1,0:T(8,128)(2,1)S(1)}, u32[]{:S(2)}, u32[]{:S(2)}) collective-permute-start(bf16[128,2560]{1,0:T(8,128)(2,1)S(1)} %add_convert_fusion.1), channel_id=1, source_target_pairs={{0,38},{1,3},{8,46},{9,11},{16,54},{17,19},{24,62},{25,27},{2,0},{... | collective-permute-start | bytes 1966088 | tf_op jit(solution)/shard_map/ppermute | solution.py:33
where the time goes:
time: 348 us; the launch traced here: 343 us
  waiting for transfers between devices  122 us (35%)
  starting transfers between devices  103 us (30%)
  Pallas kernels  95.3 us (27%)
  local copies, waits for them, and re-layouts  12.9 us (4%)
  other arithmetic  7.49 us (2%)
    ppermute x33, waiting for transfers between devices, permute(): return lax.ppermute(array, AXES, pairs)  122 us
    ppermute x33, starting transfers between devices, permute(): return lax.ppermute(array, AXES, pairs)  91 us
    pallas_call x6, Pallas kernels, choose(): pl.pallas_call(choose_kernel, in_specs=[pl.BlockSpec(memory_space=pltpu.S...  16.1 us
    pallas_call x2, Pallas kernels, select_rows(): pl.pallas_call(lambda *refs: select_kernel(scaled, *refs), grid=(width //...  13.8 us
    pallas_call x2, Pallas kernels, grad_blocks(): pl.pallas_call(grad_kernel, grid=(width // tile,), in_specs=[pl.BlockSpec...  13.5 us
    pallas_call x1, Pallas kernels, hidden_rows(): pl.pallas_call(lambda *refs: hidden_kernel(len(xs), *refs), grid=(steps,)...  13.2 us
    pallas_call x5, Pallas kernels, hold(): pl.pallas_call(lambda *refs: hold_kernel(len(arrays), start, *refs), in_s...  12.4 us
    all_to_all x2, starting transfers between devices, plane_exchange(): lax.all_to_all(rows, ('x', 'c'), split_axis=0, concat_axis=0, tiled=True)  12.1 us
  transfers between devices with their start and end apart: 35, of which 13 were waited for; matrix products, arithmetic and copies ran while one was open for 3% of the time, Pallas kernels for 23%

commit v1 on v0

--- a/solution.py
+++ b/solution.py
@@ -14,8 +14,6 @@
 beta_two = 0.95
 learn_rate = 0.003
 adam_eps = 1e-08
-
-G_CHUNKS = 2
 
 
 def flat_index(y, z, x, c):
@@ -358,10 +356,10 @@
         out[...] = grad[k * quarter : (k + 1) * quarter, :]
 
 
-def grad_blocks(where, hidden, rows, first, width, *earlier):
+def grad_blocks(where, hidden, rows, *earlier):
+    width = rows[0].shape[1]
     block = rows[0].shape[0] // 2
     tile = 256 if width % 512 else 512
-    offset = first // tile
     quarter = hidden.shape[1] // N_Y
     spec = pl.BlockSpec((quarter, tile), lambda j: (0, j))
     out = jax.ShapeDtypeStruct((quarter, width), jnp.bfloat16)
@@ -372,8 +370,8 @@
             pl.BlockSpec(memory_space=pltpu.SMEM),
             pl.BlockSpec(hidden.shape, lambda j: (0, 0)),
         ]
-        + [pl.BlockSpec((block, tile), lambda j: (0, j + offset)) for _ in range(4)]
-        + [pl.BlockSpec((4 * block, tile), lambda j: (0, j + offset))]
+        + [pl.BlockSpec((block, tile), lambda j: (0, j)) for _ in range(4)]
+        + [pl.BlockSpec((4 * block, tile), lambda j: (0, j))]
         + [pl.BlockSpec(memory_space=pl.ANY) for _ in earlier],
         out_specs=(spec,) * 4,
         out_shape=(out,) * 4,
@@ -510,9 +508,7 @@
     plan = make_plan(cap, top, here, x_parts, far_state)
     x_send = select_rows(False, cap, plan, x_parts, 0, width)
     x_rows = plane_exchange(x_send)
-    down = hold((down_weight[0],), x_parts[1])
-    partner = permute(down, lambda y, z, x, c: (y, z + 4, x, c))
-    g_parts = z_gather(hold((out_grad,), plan[0], partner))
+    g_parts = z_gather(hold((out_grad,), plan[0]))
     state = choose(bits[3], far_state, state, x_send)
     state_cores = choose(bits[0], swap(state, c=1), state, *g_parts[2:])
     state_far = swap(state_cores, zl=2)
@@ -520,7 +516,9 @@
     g_send = select_rows(True, cap, plan, g_parts, 0, width, x_rows, state_cores)
     g_rows = plane_permute(g_send)
 
-    pair = hold((down, partner), x_send)
+    down = hold((down_weight[0],), plan[0])
+    partner = permute(down, lambda y, z, x, c: (y, z + 4, x, c))
+    pair = jnp.concatenate([down, partner], axis=0)
     downs = (pair, y_move(pair, -1), y_move(pair, -2), y_move(pair, 1))
 
     hidden = hidden_rows(where, [x_rows], gate_weight[0], up_weight[0], g_send[3:])
@@ -530,27 +528,21 @@
     state = choose(bits[1], swap(state_far, zl=1), state_far)
 
     g_rows = (*g_rows, core_permute(g_rows, state_far))
-    chunk = width // G_CHUNKS
-    partials = [
-        grad_blocks(where, hidden, g_rows, i * chunk, chunk, r_send) for i in range(G_CHUNKS)
-    ]
-    grads = []
-    for i, blocks in enumerate(partials):
-        moved = [blocks[0]] + [y_move(blocks[k], k) for k in (1, 2, 3)]
-        earlier = (grads[-1], returned) if grads else (partials[-1][0],)
-        total = sum_blocks(moved, state, *earlier)
-        total = choose(bits[0], swap(total, c=1), total)
-        rows = total.shape[0] // 2
-        mine, theirs = lax.switch(
-            jump,
-            [lambda a, b, m=m: (relocate(a, m), relocate(b, m, True)) for m in jumps],
-            total[:rows],
-            total[rows:],
-        )
-        grads.append(mine.astype(jnp.float32) + theirs.astype(jnp.float32))
-    new_state = adam(jnp.concatenate(grads, axis=1), *jnp.split(state, 3, axis=0))
-
-    layer_out = z_return(*combine_rows(plan, returned, grads[0]))
+    blocks = grad_blocks(where, hidden, g_rows)
+    blocks = [blocks[0]] + [y_move(blocks[k], k) for k in (1, 2, 3)]
+    total = sum_blocks(blocks)
+    total = choose(bits[0], swap(total, c=1), total)
+    rows = total.shape[0] // 2
+    mine, theirs = lax.switch(
+        jump,
+        [lambda a, b, m=m: (relocate(a, m), relocate(b, m, True)) for m in jumps],
+        total[:rows],
+        total[rows:],
+    )
+    grad = mine.astype(jnp.float32) + theirs.astype(jnp.float32)
+    new_state = adam(grad, *jnp.split(state, 3, axis=0))
+
+    layer_out = z_return(*combine_rows(plan, returned, blocks[1]))
     return (layer_out, *new_state)
 
 

time: 348 us -> 322 us (0.925)
  starting transfers between devices: 103 us -> 89.9 us
  Pallas kernels: 95.3 us -> 85.5 us
  local copies, waits for them, and re-layouts: 12.9 us -> 9.28 us
    ppermute x33 -> x27, starting transfers between devices: 91 us -> 63.1 us  [permute(): return lax.ppermute(array, AXES, pairs)]
    ppermute x33 -> x27, waiting for transfers between devices: 122 us -> 106 us  [permute(): return lax.ppermute(array, AXES, pairs)]
    all_to_all x2, starting transfers between devices: 12.1 us -> 26.8 us  [plane_exchange(): lax.all_to_all(rows, ('x', 'c'), split_axis=0, concat_axis=0, tiled=True)]
    all_to_all x2, waiting for transfers between devices: 0.01 us -> 12.8 us  [plane_exchange(): lax.all_to_all(rows, ('x', 'c'), split_axis=0, concat_axis=0, tiled=True)]
    pallas_call x2 -> x1, Pallas kernels: 13.5 us -> 8.73 us  [grad_blocks(): pl.pallas_call(grad_kernel, grid=(width // tile,), in_specs=[pl.BlockSpec...]
    unnamed x61 -> x44, local copies, waits for them, and re-layouts: 9.85 us -> 7.16 us
    pallas_call x5 -> x4, Pallas kernels: 12.4 us -> 10.2 us  [hold(): pl.pallas_call(lambda *refs: hold_kernel(len(arrays), start, *refs), in_s...]
    pallas_call x6 -> x5, Pallas kernels: 16.1 us -> 14.9 us  [choose(): pl.pallas_call(choose_kernel, in_specs=[pl.BlockSpec(memory_space=pltpu.S...]
  transfers between devices with their start and end apart: 35 -> 29, of which waited for: 13 -> 12; matrix products, arithmetic and copies ran while one was open for 3% -> 3% of each run, Pallas kernels for 23% -> 23%
where the time goes in v1:
time: 322 us; the launch traced here: 316 us
  waiting for transfers between devices  119 us (37%)
  starting transfers between devices  89.9 us (28%)
  Pallas kernels  85.5 us (27%)
  other arithmetic  10.9 us (3%)
  local copies, waits for them, and re-layouts  9.28 us (3%)
    ppermute x27, waiting for transfers between devices, permute(): return lax.ppermute(array, AXES, pairs)  106 us
    ppermute x27, starting transfers between devices, permute(): return lax.ppermute(array, AXES, pairs)  63.1 us
    all_to_all x2, starting transfers between devices, plane_exchange(): lax.all_to_all(rows, ('x', 'c'), split_axis=0, concat_axis=0, tiled=True)  26.8 us
    pallas_call x5, Pallas kernels, choose(): pl.pallas_call(choose_kernel, in_specs=[pl.BlockSpec(memory_space=pltpu.S...  14.9 us
    pallas_call x2, Pallas kernels, select_rows(): pl.pallas_call(lambda *refs: select_kernel(scaled, *refs), grid=(width //...  13.7 us
    pallas_call x1, Pallas kernels, hidden_rows(): pl.pallas_call(lambda *refs: hidden_kernel(len(xs), *refs), grid=(steps,)...  13.2 us
    all_to_all x2, waiting for transfers between devices, plane_exchange(): lax.all_to_all(rows, ('x', 'c'), split_axis=0, concat_axis=0, tiled=True)  12.8 us
    pallas_call x4, Pallas kernels, hold(): pl.pallas_call(lambda *refs: hold_kernel(len(arrays), start, *refs), in_s...  10.2 us
  transfers between devices with their start and end apart: 29, of which 12 were waited for; matrix products, arithmetic and copies ran while one was open for 3% of the time, Pallas kernels for 23%

profile of v1, /device:TPU:1, one launch (start us, length us, event | category | flops | bytes accessed | tf_op | source)
XLA Modules:
  0.0 316.4 jit_solution(667308028996158159)
XLA Ops:
  0.7 2.6 hold.4.own
  3.2 2.0 collective-permute-start.18
  5.5 0.7 pad_add_fusion.meta
  6.2 2.1 mark.1.refs_1_.refs_2_
  8.3 5.6 %collective-permute-start.15 = (bf16[128,2688]{1,0:T(8,128)(2,1)}, bf16[128,2688]{1,0:T(8,128)(2,1)S(1)}, u32[]{:S(2)}, u32[]{:S(2)}) collective-permute-start(bf16[128,2688]{1,0:T(8,128)(2,1)} %mark.1.refs_1_.refs_2_), channel_id=1, source_target_pairs={{0,2},{1,39},{8,10},{9,47},{16,18},{17,55},{24,26},{25,63},{2,4},{... | collective-permute-start | bytes 2064392 | tf_op jit(solution)/shard_map/ppermute | solution.py:31
  13.9 14.1 %collective-permute-done.15.refs_2_.refs_3_ = bf16[128,2688]{1,0:T(8,128)(2,1)S(1)} collective-permute-done((bf16[128,2688]{1,0:T(8,128)(2,1)}, bf16[128,2688]{1,0:T(8,128)(2,1)S(1)}, u32[]{:S(2)}, u32[]{:S(2)}) %collective-permute-start.15) | collective-permute-done | bytes 688160 | tf_op jit(solution)/shard_map/ppermute | solution.py:31
  28.0 3.3 %collective-permute-start.17 = (bf16[128,2688]{1,0:T(8,128)(2,1)S(1)}, bf16[128,2688]{1,0:T(8,128)(2,1)S(1)}, u32[]{:S(2)}, u32[]{:S(2)}) collective-permute-start(bf16[128,2688]{1,0:T(8,128)(2,1)S(1)} %collective-permute-done.15.refs_2_.refs_3_), channel_id=1, source_target_pairs={{0,2},{1,39},{8,10},{9,47},{16,18},{17,55},{24,26},{25,63},{2,4},{... | collective-permute-start | bytes 2064392 | tf_op jit(solution)/shard_map/ppermute | solution.py:31
  31.6 7.6 %collective-permute-done.17.refs_4_.refs_5_ = bf16[128,2688]{1,0:T(8,128)(2,1)S(1)} collective-permute-done((bf16[128,2688]{1,0:T(8,128)(2,1)S(1)}, bf16[128,2688]{1,0:T(8,128)(2,1)S(1)}, u32[]{:S(2)}, u32[]{:S(2)}) %collective-permute-start.17) | collective-permute-done | bytes 688160 | tf_op jit(solution)/shard_map/ppermute | solution.py:31
  39.1 0.8 broadcast_in_dim.32.refs_0_
  40.6 1.7 plan.1
  42.2 7.1 %select.94.refs_0_ = bf16[8,112,2560]{2,1,0:T(8,128)(2,1)} custom-call(f32[16,512]{1,0:T(8,128)} %get-tuple-element.76.refs_0_.refs_1_.slots, f32[16,512]{1,0:T(8,128)} %get-tuple-element.77.refs_1_.weights, bf16[128,2688]{1,0:T(8,128)(2,1)} %mark.1.refs_1_.refs_2_, bf16[128,2688]{1,0:T(8,128)(2,1)} %copy-done.6, bf16[128,2688]{1,0:T(8,128)(2,1)} %copy-done.7, ...), custom_call_target="tpu_custom_call" | custom-call | flops 1 | bytes 1 | tf_op jit(solution)/shard_map/select/pallas_call | solution.py:249
  49.3 7.5 %all-to-all-start = ((bf16[8,112,2560]{2,1,0:T(8,128)(2,1)}), bf16[8,112,2560]{2,1,0:T(8,128)(2,1)}, u32[]{:S(2)}, u32[]{:S(2)}) async-start(bf16[8,112,2560]{2,1,0:T(8,128)(2,1)} %select.94.refs_0_), calls=%async_computation | async-start | bytes 9175040 | tf_op jit(solution)/shard_map/all_to_all | solution.py:448
  56.8 2.0 hold.5.refs_2_
  58.7 2.2 collective-permute-start.19
  60.9 1.8 hold.6
  62.7 2.3 collective-permute-start.23
  65.8 3.1 choose.5.own
  69.3 1.0 collective-permute-start.20
  70.3 20.2 %collective-permute-done.19.refs_3_ = bf16[128,2560]{1,0:T(8,128)(2,1)} collective-permute-done((bf16[128,2560]{1,0:T(8,128)(2,1)}, bf16[128,2560]{1,0:T(8,128)(2,1)}, u32[]{:S(2)}, u32[]{:S(2)}) %collective-permute-start.19) | collective-permute-done | bytes 655392 | tf_op jit(solution)/shard_map/ppermute | solution.py:31
  90.5 3.6 %collective-permute-start.21 = (bf16[128,2560]{1,0:T(8,128)(2,1)}, bf16[128,2560]{1,0:T(8,128)(2,1)S(1)}, u32[]{:S(2)}, u32[]{:S(2)}) collective-permute-start(bf16[128,2560]{1,0:T(8,128)(2,1)} %collective-permute-done.19.refs_3_), channel_id=1, source_target_pairs={{0,2},{1,39},{8,10},{9,47},{16,18},{17,55},{24,26},{25,63},{2,4},{... | collective-permute-start | bytes 1966088 | tf_op jit(solution)/shard_map/ppermute | solution.py:31
  94.1 2.1 pad_maximum_fusion.d0
  96.2 2.7 collective-permute-start.24
  99.2 2.8 collective-permute-done.20.refs_0_.refs_4_
  102.1 1.3 collective-permute-start.26
  103.9 0.9 copy-done.10
  104.8 1.2 copy-done.13
  105.9 3.0 choose.6.refs_7_.own
  109.0 1.5 collective-permute-start.30
  110.5 6.7 %select_scaled.1 = (bf16[224,2560]{1,0:T(8,128)(2,1)}, bf16[224,2560]{1,0:T(8,128)(2,1)}, bf16[224,2560]{1,0:T(8,128)(2,1)}, bf16[224,2560]{1,0:T(8,128)(2,1)}) custom-call(f32[16,512]{1,0:T(8,128)} %get-tuple-element.76.refs_0_.refs_1_.slots, f32[16,512]{1,0:T(8,128)} %get-tuple-element.77.refs_1_.weights, bf16[128,2560]{1,0:T(8,128)(2,1)} %hold.5.refs_2_, ...), custom_call_target="tpu_custom_call" | custom-call | flops 1 | bytes 1 | tf_op jit(solution)/shard_map/select_scaled/pallas_call | solution.py:249
  117.2 10.0 %collective-permute-start.27 = (bf16[224,2560]{1,0:T(8,128)(2,1)}, bf16[224,2560]{1,0:T(8,128)(2,1)S(1)}, u32[]{:S(2)}, u32[]{:S(2)}) collective-permute-start(bf16[224,2560]{1,0:T(8,128)(2,1)} %get-tuple-element.80), channel_id=1, source_target_pairs={{0,8},{1,9},{8,16},{9,17},{16,24},{17,25},{24,0},{25,1},{2,10},{3,... | collective-permute-start | bytes 3440648 | tf_op jit(solution)/shard_map/ppermute | solution.py:31
  127.2 2.4 collective-permute-start.28
  129.6 1.2 collective-permute-start.29
  130.8 0.6 pad_add_fusion.2.refs_0_.where
  131.4 13.2 %hidden.1 = bf16[896,768]{1,0:T(8,128)(2,1)} custom-call(s32[4]{0:T(128)} %pad_add_fusion.2.refs_0_.where, bf16[8,112,2560]{2,1,0:T(8,128)(2,1)} %all-to-all-done.refs_6_.refs_1_, bf16[2560,768]{1,0:T(8,128)(2,1)} %bitcast.20, bf16[2560,768]{1,0:T(8,128)(2,1)} %bitcast.21, bf16[224,2560]{1,0:T(8,128)(2,1)} %get-tuple-element.78.refs_4_), custom_call_target="tpu_custom_call" | custom-call | tf_op jit(solution)/shard_map/hidden/pallas_call | solution.py:303
  144.6 0.9 collective-permute-done.26.d3
  145.5 8.5 %down.1.refs_0_ = bf16[8,112,2560]{2,1,0:T(8,128)(2,1)} custom-call(bf16[896,768]{1,0:T(8,128)(2,1)} %hidden.1, bf16[192,2560]{1,0:T(8,128)(2,1)} %pad_maximum_fusion.d0, bf16[192,2560]{1,0:T(8,128)(2,1)} %collective-permute-done.24.d1, bf16[192,2560]{1,0:T(8,128)(2,1)} %collective-permute-done.25.d2, bf16[192,2560]{1,0:T(8,128)(2,1)} %collective-permute-done.26.d3), custom_call_target="tpu_custom_call" | custom-call | tf_op jit(solution)/shard_map/down/pallas_call | solution.py:328
  154.0 19.3 %all-to-all-start.1 = ((bf16[8,112,2560]{2,1,0:T(8,128)(2,1)}), bf16[8,112,2560]{2,1,0:T(8,128)(2,1)}, u32[]{:S(2)}, u32[]{:S(2)}) async-start(bf16[8,112,2560]{2,1,0:T(8,128)(2,1)} %down.1.refs_0_), calls=%async_computation.1 | async-start | bytes 9175040 | tf_op jit(solution)/shard_map/all_to_all | solution.py:448
  173.3 1.7 collective-permute-done.30.other
  175.0 3.1 choose.7.refs_4_.own
  178.1 1.0 copy-done.3
  179.5 3.8 %hold.7 = bf16[448,2560]{1,0:T(8,128)(2,1)} custom-call(bf16[224,2560]{1,0:T(8,128)(2,1)} %get-tuple-element.79.refs_0_, bf16[224,2560]{1,0:T(8,128)(2,1)} %copy-done.3, bf16[224,2560]{1,0:T(8,128)(2,1)} %copy-done.4, bf16[224,2560]{1,0:T(8,128)(2,1)} %collective-permute-done.29.refs_3_, bf16[288,2560]{1,0:T(8,128)(2,1)} %choose.7.refs_4_.own), custom_call_target="tpu_custom_call" | custom-call | flops 1 | bytes 1 | tf_op jit(solution)/shard_map/hold/pallas_call | solution.py:88
  183.3 10.6 %collective-permute-start.31 = (bf16[448,2560]{1,0:T(8,128)(2,1)}, bf16[448,2560]{1,0:T(8,128)(2,1)}, u32[]{:S(2)}, u32[]{:S(2)}) collective-permute-start(bf16[448,2560]{1,0:T(8,128)(2,1)} %hold.7), channel_id=1, source_target_pairs={{0,1},{1,0},{8,9},{9,8},{16,17},{17,16},{24,25},{25,24},{2,3},{3,2... | collective-permute-start | bytes 6881288 | tf_op jit(solution)/shard_map/ppermute | solution.py:31
  193.8 4.4 %collective-permute-done.31.refs_4_ = bf16[448,2560]{1,0:T(8,128)(2,1)} collective-permute-done((bf16[448,2560]{1,0:T(8,128)(2,1)}, bf16[448,2560]{1,0:T(8,128)(2,1)}, u32[]{:S(2)}, u32[]{:S(2)}) %collective-permute-start.31) | collective-permute-done | bytes 2293792 | tf_op jit(solution)/shard_map/ppermute | solution.py:31
  198.3 8.7 %grad.1 = (bf16[192,2560]{1,0:T(8,128)(2,1)}, bf16[192,2560]{1,0:T(8,128)(2,1)}, bf16[192,2560]{1,0:T(8,128)(2,1)}, bf16[192,2560]{1,0:T(8,128)(2,1)}) custom-call(s32[4]{0:T(128)} %pad_add_fusion.2.refs_0_.where, bf16[896,768]{1,0:T(8,128)(2,1)} %hidden.1, bf16[224,2560]{1,0:T(8,128)(2,1)} %get-tuple-element.79.refs_0_, bf16[224,2560]{1,0:T(8,128)(2,1)} %copy-done.3, ...), custom_call_target="tpu_custom_call" | custom-call | tf_op jit(solution)/shard_map/grad/pallas_call | solution.py:366
  207.0 2.8 collective-permute-start.36
  209.8 4.5 %collective-permute-start.37 = (bf16[192,2560]{1,0:T(8,128)(2,1)}, bf16[192,2560]{1,0:T(8,128)(2,1)S(1)}, u32[]{:S(2)}, u32[]{:S(2)}) collective-permute-start(bf16[192,2560]{1,0:T(8,128)(2,1)} %get-tuple-element.88), channel_id=1, source_target_pairs={{0,128},{1,129},{8,136},{9,137},{16,144},{17,145},{24,152},{25,153... | collective-permute-start | bytes 2949128 | tf_op jit(solution)/shard_map/ppermute | solution.py:31
  214.3 12.8 %all-to-all-done.1.rows = bf16[8,112,2560]{2,1,0:T(8,128)(2,1)} async-done(((bf16[8,112,2560]{2,1,0:T(8,128)(2,1)}), bf16[8,112,2560]{2,1,0:T(8,128)(2,1)}, u32[]{:S(2)}, u32[]{:S(2)}) %all-to-all-start.1) | async-done | bytes 4587552 | tf_op jit(solution)/shard_map/all_to_all | solution.py:448
  227.1 25.4 %collective-permute-done.32.refs_0_.b = bf16[192,2560]{1,0:T(8,128)(2,1)S(1)} collective-permute-done((bf16[192,2560]{1,0:T(8,128)(2,1)}, bf16[192,2560]{1,0:T(8,128)(2,1)S(1)}, u32[]{:S(2)}, u32[]{:S(2)}) %collective-permute-start.32) | collective-permute-done | bytes 983072 | tf_op jit(solution)/shard_map/ppermute | solution.py:31
  252.4 1.0 copy-done.5
  253.4 9.0 %combine.1 = (f32[128,2560]{1,0:T(8,128)}, bf16[128,2560]{1,0:T(8,128)(2,1)}, bf16[128,2560]{1,0:T(8,128)(2,1)}, bf16[128,2560]{1,0:T(8,128)(2,1)}) custom-call(f32[16,512]{1,0:T(8,128)} %get-tuple-element.76.refs_0_.refs_1_.slots, f32[16,512]{1,0:T(8,128)} %get-tuple-element.77.refs_1_.weights, bf16[8,112,2560]{2,1,0:T(8,128)(2,1)} %all-to-all-done.1.rows, ...), custom_call_target="tpu_custom_call" | custom-call | tf_op jit(solution)/shard_map/combine/pallas_call | solution.py:416
  262.4 1.0 copy-done.15
  263.4 3.5 %sum.1.own = bf16[192,2560]{1,0:T(8,128)(2,1)} custom-call(bf16[192,2560]{1,0:T(8,128)(2,1)} %get-tuple-element.87.a, bf16[192,2560]{1,0:T(8,128)(2,1)} %copy-done.5, bf16[192,2560]{1,0:T(8,128)(2,1)} %copy-done.15, bf16[192,2560]{1,0:T(8,128)(2,1)} %collective-permute-done.38.d), custom_call_target="tpu_custom_call" | custom-call | flops 1 | bytes 1 | tf_op jit(solution)/shard_map/sum/pallas_call | solution.py:157
  267.0 1.2 collective-permute-start.39
  268.2 3.1 choose.8
  271.4 1.4 collective-permute-start.35
  273.4 2.1 add_convert_fusion.1
  275.5 0.9 copy-done.16
  276.4 2.5 choose.9
  278.9 1.2 fusion.12
  280.2 30.7 %conditional.4 = (bf16[96,2560]{1,0:T(8,128)(2,1)S(1)}, bf16[96,2560]{1,0:T(8,128)(2,1)}) conditional(s32[]{:T(128)} %clamp.3, (bf16[96,2560]{1,0:T(8,128)(2,1)S(1)}, bf16[96,2560]{1,0:T(8,128)(2,1)S(1)}) %tuple.74, (bf16[96,2560]{1,0:T(8,128)(2,1)S(1)}, bf16[96,2560]{1,0:T(8,128)(2,1)S(1)}) %fusion.12, ...), branch_computations={%region_1.2_spmd, %region_2.3_spmd, %region_3.4_spmd, %region_4.5_... | conditional | bytes 4915296
  280.2 2.7 collective-permute-start.9
  282.9 27.9 %collective-permute-done.9 = bf16[96,2560]{1,0:T(8,128)(2,1)S(1)} collective-permute-done((bf16[96,2560]{1,0:T(8,128)(2,1)S(1)}, bf16[96,2560]{1,0:T(8,128)(2,1)S(1)}, u32[]{:S(2)}, u32[]{:S(2)}) %collective-permute-start.9) | collective-permute-done | bytes 491552 | tf_op jit(solution)/shard_map/cond/branch_5_fun/ppermute | solution.py:31
  310.9 2.9 fusion.4
  313.8 2.2 add_convert_fusion
  (72 shorter events, 3.7 us)
Async XLA Ops:
  0.6 4.6 %copy-start.19 = (s32[128,6]{0,1:T(8,128)S(1)}, s32[128,6]{0,1:T(8,128)}, u32[]{:S(2)}) copy-start(s32[128,6]{0,1:T(8,128)} %param.20) | copy-start | bytes 9220
  0.6 4.7 %copy-start.18 = (f32[128,6]{0,1:T(8,128)S(1)}, f32[128,6]{0,1:T(8,128)}, u32[]{:S(2)}) copy-start(f32[128,6]{0,1:T(8,128)} %param.21) | copy-start | bytes 9220
  3.2 28.2 %copy-start.20 = (s32[32]{0:T(128)S(1)}, s32[32]{0:T(128)}, u32[]{:S(2)}) copy-start(s32[32]{0:T(128)} %param.22) | copy-start | bytes 388
  3.2 35.9 %collective-permute-start.18 = (bf16[288,2560]{1,0:T(8,128)(2,1)}, bf16[288,2560]{1,0:T(8,128)(2,1)S(1)}, u32[]{:S(2)}, u32[]{:S(2)}) collective-permute-start(bf16[288,2560]{1,0:T(8,128)(2,1)} %hold.4.own), channel_id=1, source_target_pairs={{0,8},{1,9},{8,0},{9,1},{16,24},{17,25},{24,16},{25,17},{2,10},{3,... | collective-permute-start | bytes 4423688 | tf_op jit(solution)/shard_map/ppermute | solution.py:31
  8.3 19.7 %collective-permute-start.15 = (bf16[128,2688]{1,0:T(8,128)(2,1)}, bf16[128,2688]{1,0:T(8,128)(2,1)S(1)}, u32[]{:S(2)}, u32[]{:S(2)}) collective-permute-start(bf16[128,2688]{1,0:T(8,128)(2,1)} %mark.1.refs_1_.refs_2_), channel_id=1, source_target_pairs={{0,2},{1,39},{8,10},{9,47},{16,18},{17,55},{24,26},{25,63},{2,4},{... | collective-permute-start | bytes 2064392 | tf_op jit(solution)/shard_map/ppermute | solution.py:31
  13.9 17.7 %collective-permute-start.16 = (bf16[128,2688]{1,0:T(8,128)(2,1)}, bf16[128,2688]{1,0:T(8,128)(2,1)S(1)}, u32[]{:S(2)}, u32[]{:S(2)}) collective-permute-start(bf16[128,2688]{1,0:T(8,128)(2,1)} %mark.1.refs_1_.refs_2_), channel_id=1, source_target_pairs={{0,38},{1,3},{8,46},{9,11},{16,54},{17,19},{24,62},{25,27},{2,0},{... | collective-permute-start | bytes 2064392 | tf_op jit(solution)/shard_map/ppermute | solution.py:31
  27.9 12.0 %copy-start.6 = (bf16[128,2688]{1,0:T(8,128)(2,1)}, bf16[128,2688]{1,0:T(8,128)(2,1)S(1)}, u32[]{:S(2)}) copy-start(bf16[128,2688]{1,0:T(8,128)(2,1)S(1)} %collective-permute-done.15.refs_2_.refs_3_) | copy-start | bytes 2064388
  28.0 11.2 %collective-permute-start.17 = (bf16[128,2688]{1,0:T(8,128)(2,1)S(1)}, bf16[128,2688]{1,0:T(8,128)(2,1)S(1)}, u32[]{:S(2)}, u32[]{:S(2)}) collective-permute-start(bf16[128,2688]{1,0:T(8,128)(2,1)S(1)} %collective-permute-done.15.refs_2_.refs_3_), channel_id=1, source_target_pairs={{0,2},{1,39},{8,10},{9,47},{16,18},{17,55},{24,26},{25,63},{2,4},{... | collective-permute-start | bytes 2064392 | tf_op jit(solution)/shard_map/ppermute | solution.py:31
  31.6 8.3 %copy-start.7 = (bf16[128,2688]{1,0:T(8,128)(2,1)}, bf16[128,2688]{1,0:T(8,128)(2,1)S(1)}, u32[]{:S(2)}) copy-start(bf16[128,2688]{1,0:T(8,128)(2,1)S(1)} %collective-permute-done.16.refs_3_.refs_4_) | copy-start | bytes 2064388
  39.1 0.9 copy-start.8
  39.1 1.4 copy-start.1
  49.3 61.2 %all-to-all-start = ((bf16[8,112,2560]{2,1,0:T(8,128)(2,1)}), bf16[8,112,2560]{2,1,0:T(8,128)(2,1)}, u32[]{:S(2)}, u32[]{:S(2)}) async-start(bf16[8,112,2560]{2,1,0:T(8,128)(2,1)} %select.94.refs_0_), calls=%async_computation | async-start | bytes 9175040 | tf_op jit(solution)/shard_map/all_to_all | solution.py:448
  58.7 31.8 %collective-permute-start.19 = (bf16[128,2560]{1,0:T(8,128)(2,1)}, bf16[128,2560]{1,0:T(8,128)(2,1)}, u32[]{:S(2)}, u32[]{:S(2)}) collective-permute-start(bf16[128,2560]{1,0:T(8,128)(2,1)} %hold.5.refs_2_), channel_id=1, source_target_pairs={{0,2},{1,39},{8,10},{9,47},{16,18},{17,55},{24,26},{25,63},{2,4},{... | collective-permute-start | bytes 1966088 | tf_op jit(solution)/shard_map/ppermute | solution.py:31
  62.7 31.4 %collective-permute-start.23 = (bf16[96,2560]{1,0:T(8,128)(2,1)}, bf16[96,2560]{1,0:T(8,128)(2,1)}, u32[]{:S(2)}, u32[]{:S(2)}) collective-permute-start(bf16[96,2560]{1,0:T(8,128)(2,1)} %hold.6), channel_id=1, source_target_pairs={{0,32},{1,33},{8,40},{9,41},{16,48},{17,49},{24,56},{25,57},{2,34}... | collective-permute-start | bytes 1474568 | tf_op jit(solution)/shard_map/ppermute | solution.py:31
  65.7 3.6 %copy-start.11 = (bf16[128,2560]{1,0:T(8,128)(2,1)S(1)}, bf16[128,2560]{1,0:T(8,128)(2,1)}, u32[]{:S(2)}) copy-start(bf16[128,2560]{1,0:T(8,128)(2,1)} %hold.5.refs_2_) | copy-start | bytes 1966084
  65.8 28.3 %copy-start.12 = (bf16[96,2560]{1,0:T(8,128)(2,1)S(1)}, bf16[96,2560]{1,0:T(8,128)(2,1)}, u32[]{:S(2)}) copy-start(bf16[96,2560]{1,0:T(8,128)(2,1)} %hold.6) | copy-start | bytes 1474564
  68.9 35.0 %collective-permute-start.22 = (bf16[288,2560]{1,0:T(8,128)(2,1)}, bf16[288,2560]{1,0:T(8,128)(2,1)S(1)}, u32[]{:S(2)}, u32[]{:S(2)}) collective-permute-start(bf16[288,2560]{1,0:T(8,128)(2,1)} %choose.5.own), channel_id=1, source_target_pairs={{0,1},{1,0},{8,9},{9,8},{16,17},{17,16},{24,25},{25,24},{2,3},{3,2... | collective-permute-start | bytes 4423688 | tf_op jit(solution)/shard_map/ppermute | solution.py:31
  69.3 32.7 %collective-permute-start.20 = (bf16[128,2560]{1,0:T(8,128)(2,1)S(1)}, bf16[128,2560]{1,0:T(8,128)(2,1)S(1)}, u32[]{:S(2)}, u32[]{:S(2)}) collective-permute-start(bf16[128,2560]{1,0:T(8,128)(2,1)S(1)} %copy-done.11), channel_id=1, source_target_pairs={{0,38},{1,3},{8,46},{9,11},{16,54},{17,19},{24,62},{25,27},{2,0},{... | collective-permute-start | bytes 1966088 | tf_op jit(solution)/shard_map/ppermute | solution.py:31
  90.5 13.4 %collective-permute-start.21 = (bf16[128,2560]{1,0:T(8,128)(2,1)}, bf16[128,2560]{1,0:T(8,128)(2,1)S(1)}, u32[]{:S(2)}, u32[]{:S(2)}) collective-permute-start(bf16[128,2560]{1,0:T(8,128)(2,1)} %collective-permute-done.19.refs_3_), channel_id=1, source_target_pairs={{0,2},{1,39},{8,10},{9,47},{16,18},{17,55},{24,26},{25,63},{2,4},{... | collective-permute-start | bytes 1966088 | tf_op jit(solution)/shard_map/ppermute | solution.py:31
  96.2 31.0 %collective-permute-start.24 = (bf16[192,2560]{1,0:T(8,128)(2,1)}, bf16[192,2560]{1,0:T(8,128)(2,1)}, u32[]{:S(2)}, u32[]{:S(2)}) collective-permute-start(bf16[192,2560]{1,0:T(8,128)(2,1)} %pad_maximum_fusion.d0), channel_id=1, source_target_pairs={{0,192},{1,193},{8,200},{9,201},{16,208},{17,209},{24,216},{25,217... | collective-permute-start | bytes 2949128 | tf_op jit(solution)/shard_map/ppermute | solution.py:31
  98.9 30.7 %collective-permute-start.25 = (bf16[192,2560]{1,0:T(8,128)(2,1)}, bf16[192,2560]{1,0:T(8,128)(2,1)}, u32[]{:S(2)}, u32[]{:S(2)}) collective-permute-start(bf16[192,2560]{1,0:T(8,128)(2,1)} %pad_maximum_fusion.d0), channel_id=1, source_target_pairs={{0,128},{1,129},{8,136},{9,137},{16,144},{17,145},{24,152},{25,153... | collective-permute-start | bytes 2949128 | tf_op jit(solution)/shard_map/ppermute | solution.py:31
  102.1 1.8 copy-start.9
  102.1 43.5 %collective-permute-start.26 = (bf16[192,2560]{1,0:T(8,128)(2,1)}, bf16[192,2560]{1,0:T(8,128)(2,1)}, u32[]{:S(2)}, u32[]{:S(2)}) collective-permute-start(bf16[192,2560]{1,0:T(8,128)(2,1)} %pad_maximum_fusion.d0), channel_id=1, source_target_pairs={{0,64},{1,65},{8,72},{9,73},{16,80},{17,81},{24,88},{25,89},{2,66}... | collective-permute-start | bytes 2949128 | tf_op jit(solution)/shard_map/ppermute | solution.py:31
  103.9 0.9 copy-start.10
  104.7 1.2 copy-start.13
  109.0 66.0 %collective-permute-start.30 = (bf16[288,2560]{1,0:T(8,128)(2,1)}, bf16[288,2560]{1,0:T(8,128)(2,1)}, u32[]{:S(2)}, u32[]{:S(2)}) collective-permute-start(bf16[288,2560]{1,0:T(8,128)(2,1)} %choose.6.refs_7_.own), channel_id=1, source_target_pairs={{0,4},{1,5},{8,12},{9,13},{16,20},{17,21},{24,28},{25,29},{2,6},{3... | collective-permute-start | bytes 4423688 | tf_op jit(solution)/shard_map/ppermute | solution.py:31
  117.2 60.9 %collective-permute-start.27 = (bf16[224,2560]{1,0:T(8,128)(2,1)}, bf16[224,2560]{1,0:T(8,128)(2,1)S(1)}, u32[]{:S(2)}, u32[]{:S(2)}) collective-permute-start(bf16[224,2560]{1,0:T(8,128)(2,1)} %get-tuple-element.80), channel_id=1, source_target_pairs={{0,8},{1,9},{8,16},{9,17},{16,24},{17,25},{24,0},{25,1},{2,10},{3,... | collective-permute-start | bytes 3440648 | tf_op jit(solution)/shard_map/ppermute | solution.py:31
  127.2 50.9 %collective-permute-start.28 = (bf16[224,2560]{1,0:T(8,128)(2,1)}, bf16[224,2560]{1,0:T(8,128)(2,1)S(1)}, u32[]{:S(2)}, u32[]{:S(2)}) collective-permute-start(bf16[224,2560]{1,0:T(8,128)(2,1)} %get-tuple-element.81), channel_id=1, source_target_pairs={{0,16},{1,17},{8,24},{9,25},{16,0},{17,1},{24,8},{25,9},{2,18},{3,... | collective-permute-start | bytes 3440648 | tf_op jit(solution)/shard_map/ppermute | solution.py:31
  129.6 48.5 %collective-permute-start.29 = (bf16[224,2560]{1,0:T(8,128)(2,1)}, bf16[224,2560]{1,0:T(8,128)(2,1)}, u32[]{:S(2)}, u32[]{:S(2)}) collective-permute-start(bf16[224,2560]{1,0:T(8,128)(2,1)} %get-tuple-element.78.refs_4_), channel_id=1, source_target_pairs={{0,24},{1,25},{8,0},{9,1},{16,8},{17,9},{24,16},{25,17},{2,26},{3,... | collective-permute-start | bytes 3440648 | tf_op jit(solution)/shard_map/ppermute | solution.py:31
  154.0 73.0 %all-to-all-start.1 = ((bf16[8,112,2560]{2,1,0:T(8,128)(2,1)}), bf16[8,112,2560]{2,1,0:T(8,128)(2,1)}, u32[]{:S(2)}, u32[]{:S(2)}) async-start(bf16[8,112,2560]{2,1,0:T(8,128)(2,1)} %down.1.refs_0_), calls=%async_computation.1 | async-start | bytes 9175040 | tf_op jit(solution)/shard_map/all_to_all | solution.py:448
  178.1 1.0 copy-start.3
  178.1 1.4 copy-start.4
  183.3 23.8 %copy-start = (bf16[288,2560]{1,0:T(8,128)(2,1)S(1)}, bf16[288,2560]{1,0:T(8,128)(2,1)}, u32[]{:S(2)}) copy-start(bf16[288,2560]{1,0:T(8,128)(2,1)} %choose.7.refs_4_.own) | copy-start | bytes 4423684
  183.3 15.0 %collective-permute-start.31 = (bf16[448,2560]{1,0:T(8,128)(2,1)}, bf16[448,2560]{1,0:T(8,128)(2,1)}, u32[]{:S(2)}, u32[]{:S(2)}) collective-permute-start(bf16[448,2560]{1,0:T(8,128)(2,1)} %hold.7), channel_id=1, source_target_pairs={{0,1},{1,0},{8,9},{9,8},{16,17},{17,16},{24,25},{25,24},{2,3},{3,2... | collective-permute-start | bytes 6881288 | tf_op jit(solution)/shard_map/ppermute | solution.py:31
  207.0 45.5 %collective-permute-start.32 = (bf16[192,2560]{1,0:T(8,128)(2,1)}, bf16[192,2560]{1,0:T(8,128)(2,1)S(1)}, u32[]{:S(2)}, u32[]{:S(2)}) collective-permute-start(bf16[192,2560]{1,0:T(8,128)(2,1)} %get-tuple-element.82), channel_id=1, source_target_pairs={{0,64},{1,65},{8,72},{9,73},{16,80},{17,81},{24,88},{25,89},{2,66}... | collective-permute-start | bytes 2949128 | tf_op jit(solution)/shard_map/ppermute | solution.py:31
  207.0 61.2 %collective-permute-start.36 = (bf16[288,2560]{1,0:T(8,128)(2,1)S(1)}, bf16[288,2560]{1,0:T(8,128)(2,1)}, u32[]{:S(2)}, u32[]{:S(2)}) collective-permute-start(bf16[288,2560]{1,0:T(8,128)(2,1)S(1)} %copy-done), channel_id=1, source_target_pairs={{0,2},{1,3},{8,10},{9,11},{16,18},{17,19},{24,26},{25,27},{2,0},{3... | collective-permute-start | bytes 4423688 | tf_op jit(solution)/shard_map/ppermute | solution.py:31
  209.8 52.6 %collective-permute-start.37 = (bf16[192,2560]{1,0:T(8,128)(2,1)}, bf16[192,2560]{1,0:T(8,128)(2,1)S(1)}, u32[]{:S(2)}, u32[]{:S(2)}) collective-permute-start(bf16[192,2560]{1,0:T(8,128)(2,1)} %get-tuple-element.88), channel_id=1, source_target_pairs={{0,128},{1,129},{8,136},{9,137},{16,144},{17,145},{24,152},{25,153... | collective-permute-start | bytes 2949128 | tf_op jit(solution)/shard_map/ppermute | solution.py:31
  214.3 48.1 %collective-permute-start.38 = (bf16[192,2560]{1,0:T(8,128)(2,1)}, bf16[192,2560]{1,0:T(8,128)(2,1)}, u32[]{:S(2)}, u32[]{:S(2)}) collective-permute-start(bf16[192,2560]{1,0:T(8,128)(2,1)} %get-tuple-element.89), channel_id=1, source_target_pairs={{0,192},{1,193},{8,200},{9,201},{16,208},{17,209},{24,216},{25,217... | collective-permute-start | bytes 2949128 | tf_op jit(solution)/shard_map/ppermute | solution.py:31
  252.4 1.0 copy-start.5
  262.4 11.0 %collective-permute-start.33 = (bf16[128,2560]{1,0:T(8,128)(2,1)}, bf16[128,2560]{1,0:T(8,128)(2,1)}, u32[]{:S(2)}, u32[]{:S(2)}) collective-permute-start(bf16[128,2560]{1,0:T(8,128)(2,1)} %get-tuple-element.84), channel_id=1, source_target_pairs={{0,38},{1,3},{8,46},{9,11},{16,54},{17,19},{24,62},{25,27},{2,0},{... | collective-permute-start | bytes 1966088 | tf_op jit(solution)/shard_map/ppermute | solution.py:31
  262.4 1.0 copy-start.15
  267.0 8.5 %collective-permute-start.39 = (bf16[192,2560]{1,0:T(8,128)(2,1)}, bf16[192,2560]{1,0:T(8,128)(2,1)S(1)}, u32[]{:S(2)}, u32[]{:S(2)}) collective-permute-start(bf16[192,2560]{1,0:T(8,128)(2,1)} %sum.1.own), channel_id=1, source_target_pairs={{0,1},{1,0},{8,9},{9,8},{16,17},{17,16},{24,25},{25,24},{2,3},{3,2... | collective-permute-start | bytes 2949128 | tf_op jit(solution)/shard_map/ppermute | solution.py:31
  268.2 5.2 %copy-start.17 = (bf16[128,2560]{1,0:T(8,128)(2,1)S(1)}, bf16[128,2560]{1,0:T(8,128)(2,1)}, u32[]{:S(2)}) copy-start(bf16[128,2560]{1,0:T(8,128)(2,1)} %get-tuple-element.85) | copy-start | bytes 1966084
  271.4 42.5 %collective-permute-start.35 = (bf16[128,2560]{1,0:T(8,128)(2,1)}, bf16[128,2560]{1,0:T(8,128)(2,1)S(1)}, u32[]{:S(2)}, u32[]{:S(2)}) collective-permute-start(bf16[128,2560]{1,0:T(8,128)(2,1)} %get-tuple-element.86), channel_id=1, source_target_pairs={{0,2},{1,39},{8,10},{9,47},{16,18},{17,55},{24,26},{25,63},{2,4},{... | collective-permute-start | bytes 1966088 | tf_op jit(solution)/shard_map/ppermute | solution.py:31
  275.5 38.4 %collective-permute-start.34 = (bf16[128,2560]{1,0:T(8,128)(2,1)}, bf16[128,2560]{1,0:T(8,128)(2,1)}, u32[]{:S(2)}, u32[]{:S(2)}) collective-permute-start(bf16[128,2560]{1,0:T(8,128)(2,1)} %add_convert_fusion.1), channel_id=1, source_target_pairs={{0,38},{1,3},{8,46},{9,11},{16,54},{17,19},{24,62},{25,27},{2,0},{... | collective-permute-start | bytes 1966088 | tf_op jit(solution)/shard_map/ppermute | solution.py:31
  275.5 0.9 copy-start.16
  280.2 30.7 %copy-start.2 = (bf16[288,2560]{1,0:T(8,128)(2,1)S(1)}, bf16[288,2560]{1,0:T(8,128)(2,1)}, u32[]{:S(2)}) copy-start(bf16[288,2560]{1,0:T(8,128)(2,1)} %choose.8) | copy-start | bytes 4423684
  280.2 30.6 %collective-permute-start.9 = (bf16[96,2560]{1,0:T(8,128)(2,1)S(1)}, bf16[96,2560]{1,0:T(8,128)(2,1)S(1)}, u32[]{:S(2)}, u32[]{:S(2)}) collective-permute-start(bf16[96,2560]{1,0:T(8,128)(2,1)S(1)} %get-tuple-element.50), channel_id=1, source_target_pairs={{0,10},{1,11},{8,2},{9,3},{16,26},{17,27},{24,18},{25,19},{2,8},{3... | collective-permute-start | bytes 1474568 | tf_op jit(solution)/shard_map/cond/branch_5_fun/ppermute | solution.py:31
  282.9 28.0 %collective-permute-start.10 = (bf16[96,2560]{1,0:T(8,128)(2,1)S(1)}, bf16[96,2560]{1,0:T(8,128)(2,1)}, u32[]{:S(2)}, u32[]{:S(2)}) collective-permute-start(bf16[96,2560]{1,0:T(8,128)(2,1)S(1)} %get-tuple-element.51), channel_id=1, source_target_pairs={{0,42},{1,43},{8,34},{9,35},{16,58},{17,59},{24,50},{25,51},{2,40}... | collective-permute-start | bytes 1474568 | tf_op jit(solution)/shard_map/cond/branch_5_fun/ppermute | solution.py:31
  310.9 2.9 copy-start.14

commit v2 on v1

--- a/solution.py
+++ b/solution.py
@@ -448,12 +448,25 @@
     return lax.all_to_all(rows, ("x", "c"), split_axis=0, concat_axis=0, tiled=True)
 
 
-def z_return(own, near, other, far):
-    step = z_down(far).astype(jnp.float32) + near.astype(jnp.float32)
+def total_kernel(own, near, other, *refs):
+    total = own[...] + near[...].astype(jnp.float32) + other[...].astype(jnp.float32)
+    refs[-1][...] = total.astype(jnp.bfloat16)
+
+
+def z_return(own, near, other, far_back, *earlier):
+    step = far_back.astype(jnp.float32) + near.astype(jnp.float32)
     from_near = z_down(step.astype(jnp.bfloat16))
     from_other = z_up(other)
-    total = own + from_near.astype(jnp.float32) + from_other.astype(jnp.float32)
-    return total.astype(jnp.bfloat16)
+    return pl.pallas_call(
+        total_kernel,
+        in_specs=[pl.BlockSpec(memory_space=pltpu.VMEM) for _ in range(3)]
+        + [pl.BlockSpec(memory_space=pl.ANY) for _ in earlier],
+        out_specs=pl.BlockSpec(memory_space=pltpu.VMEM),
+        out_shape=jax.ShapeDtypeStruct(own.shape, jnp.bfloat16),
+        compiler_params=params(60),
+        cost_estimate=LIGHT,
+        name="total",
+    )(own, from_near, from_other, *earlier)
 
 
 def y_move(array, k):
@@ -525,24 +538,26 @@
     r_send = down_rows(hidden, downs, cap, 0, width)
     returned = plane_exchange(r_send)
     state_far = choose(bits[2], state_far, state_cores, r_send)
-    state = choose(bits[1], swap(state_far, zl=1), state_far)
+    state_near = swap(state_far, zl=1)
 
     g_rows = (*g_rows, core_permute(g_rows, state_far))
     blocks = grad_blocks(where, hidden, g_rows)
     blocks = [blocks[0]] + [y_move(blocks[k], k) for k in (1, 2, 3)]
-    total = sum_blocks(blocks)
-    total = choose(bits[0], swap(total, c=1), total)
-    rows = total.shape[0] // 2
+    combined = combine_rows(plan, returned, blocks[1])
+    far_back = z_down(combined[3])
+    total = sum_blocks(blocks, far_back)
+    other = swap(total, c=1)
+    halves = [jnp.where(bits[0] == 1, o, t) for o, t in zip(jnp.split(other, 2), jnp.split(total, 2))]
     mine, theirs = lax.switch(
         jump,
         [lambda a, b, m=m: (relocate(a, m), relocate(b, m, True)) for m in jumps],
-        total[:rows],
-        total[rows:],
+        *halves,
     )
     grad = mine.astype(jnp.float32) + theirs.astype(jnp.float32)
+    state = jnp.where(bits[1] == 1, state_near, state_far)
     new_state = adam(grad, *jnp.split(state, 3, axis=0))
 
-    layer_out = z_return(*combine_rows(plan, returned, blocks[1]))
+    layer_out = z_return(*combined[:3], far_back, theirs)
     return (layer_out, *new_state)
 
 

time: 322 us -> 318 us (0.988)
  the two profiles are of different devices: /device:TPU:1 before, /device:TPU:48 now
where the time goes in v2:
time: 318 us; the launch traced here: 316 us
  waiting for transfers between devices  148 us (47%)
  Pallas kernels  82.7 us (26%)
  starting transfers between devices  66.8 us (21%)
  other arithmetic  9.34 us (3%)
  local copies, waits for them, and re-layouts  7.89 us (2%)
    ppermute x27, waiting for transfers between devices, permute(): return lax.ppermute(array, AXES, pairs)  134 us
    ppermute x27, starting transfers between devices, permute(): return lax.ppermute(array, AXES, pairs)  57 us
    all_to_all x2, waiting for transfers between devices, plane_exchange(): lax.all_to_all(rows, ('x', 'c'), split_axis=0, concat_axis=0, tiled=True)  14 us
    pallas_call x2, Pallas kernels, select_rows(): pl.pallas_call(lambda *refs: select_kernel(scaled, *refs), grid=(width //...  13.8 us
    pallas_call x1, Pallas kernels, hidden_rows(): pl.pallas_call(lambda *refs: hidden_kernel(len(xs), *refs), grid=(steps,)...  13.2 us
    pallas_call x4, Pallas kernels, hold(): pl.pallas_call(lambda *refs: hold_kernel(len(arrays), start, *refs), in_s...  10.2 us
    all_to_all x2, starting transfers between devices, plane_exchange(): lax.all_to_all(rows, ('x', 'c'), split_axis=0, concat_axis=0, tiled=True)  9.79 us
    pallas_call x3, Pallas kernels, choose(): pl.pallas_call(choose_kernel, in_specs=[pl.BlockSpec(memory_space=pltpu.S...  9.21 us
  transfers between devices with their start and end apart: 29, of which 13 were waited for; matrix products, arithmetic and copies ran while one was open for 3% of the time, Pallas kernels for 22%

profile of v2, /device:TPU:48, one launch (start us, length us, event | category | flops | bytes accessed | tf_op | source)
XLA Modules:
  0.0 316.4 jit_solution(2298634417905996869)
XLA Ops:
  0.7 2.6 hold.4.own
  3.2 1.5 collective-permute-start.18
  4.9 0.7 pad_add_fusion.meta
  5.7 2.1 mark.1.refs_1_.refs_2_
  7.7 1.9 collective-permute-start.15
  9.8 14.6 %collective-permute-done.15.refs_2_.refs_3_ = bf16[128,2688]{1,0:T(8,128)(2,1)S(1)} collective-permute-done((bf16[128,2688]{1,0:T(8,128)(2,1)}, bf16[128,2688]{1,0:T(8,128)(2,1)S(1)}, u32[]{:S(2)}, u32[]{:S(2)}) %collective-permute-start.15) | collective-permute-done | bytes 688160 | tf_op jit(solution)/shard_map/ppermute | solution.py:31
  24.4 2.4 collective-permute-start.17
  27.1 10.4 %collective-permute-done.17.refs_4_.refs_5_ = bf16[128,2688]{1,0:T(8,128)(2,1)S(1)} collective-permute-done((bf16[128,2688]{1,0:T(8,128)(2,1)S(1)}, bf16[128,2688]{1,0:T(8,128)(2,1)S(1)}, u32[]{:S(2)}, u32[]{:S(2)}) %collective-permute-start.17) | collective-permute-done | bytes 688160 | tf_op jit(solution)/shard_map/ppermute | solution.py:31
  37.5 0.8 broadcast_in_dim.51.refs_0_
  38.9 1.7 plan.1
  40.6 7.1 %select.94.refs_0_ = bf16[8,112,2560]{2,1,0:T(8,128)(2,1)} custom-call(f32[16,512]{1,0:T(8,128)} %get-tuple-element.68.refs_0_.refs_1_.slots, f32[16,512]{1,0:T(8,128)} %get-tuple-element.69.refs_1_.weights, bf16[128,2688]{1,0:T(8,128)(2,1)} %mark.1.refs_1_.refs_2_, bf16[128,2688]{1,0:T(8,128)(2,1)} %copy-done.6, bf16[128,2688]{1,0:T(8,128)(2,1)} %copy-done.7, ...), custom_call_target="tpu_custom_call" | custom-call | flops 1 | bytes 1 | tf_op jit(solution)/shard_map/select/pallas_call | solution.py:249
  47.7 4.6 %all-to-all-start = ((bf16[8,112,2560]{2,1,0:T(8,128)(2,1)}), bf16[8,112,2560]{2,1,0:T(8,128)(2,1)}, u32[]{:S(2)}, u32[]{:S(2)}) async-start(bf16[8,112,2560]{2,1,0:T(8,128)(2,1)} %select.94.refs_0_), calls=%async_computation | async-start | bytes 9175040 | tf_op jit(solution)/shard_map/all_to_all | solution.py:448
  52.3 2.0 hold.5.refs_2_
  54.3 1.6 collective-permute-start.19
  55.9 1.8 hold.6
  57.8 5.4 %collective-permute-start.23 = (bf16[96,2560]{1,0:T(8,128)(2,1)}, bf16[96,2560]{1,0:T(8,128)(2,1)}, u32[]{:S(2)}, u32[]{:S(2)}) collective-permute-start(bf16[96,2560]{1,0:T(8,128)(2,1)} %hold.6), channel_id=1, source_target_pairs={{0,32},{1,33},{8,40},{9,41},{16,48},{17,49},{24,56},{25,57},{2,34}... | collective-permute-start | bytes 1474568 | tf_op jit(solution)/shard_map/ppermute | solution.py:31
  63.9 3.1 choose.3.own
  67.0 0.8 collective-permute-start.22
  68.0 3.0 collective-permute-done.19.refs_3_
  71.1 15.7 %collective-permute-done.23 = bf16[96,2560]{1,0:T(8,128)(2,1)} collective-permute-done((bf16[96,2560]{1,0:T(8,128)(2,1)}, bf16[96,2560]{1,0:T(8,128)(2,1)}, u32[]{:S(2)}, u32[]{:S(2)}) %collective-permute-start.23) | collective-permute-done | bytes 491552 | tf_op jit(solution)/shard_map/ppermute | solution.py:31
  86.7 2.1 pad_maximum_fusion.d0
  89.3 2.9 collective-permute-start.25
  92.2 9.1 %collective-permute-done.20.refs_0_.refs_4_ = bf16[128,2560]{1,0:T(8,128)(2,1)S(1)} collective-permute-done((bf16[128,2560]{1,0:T(8,128)(2,1)S(1)}, bf16[128,2560]{1,0:T(8,128)(2,1)S(1)}, u32[]{:S(2)}, u32[]{:S(2)}) %collective-permute-start.20) | collective-permute-done | bytes 655392 | tf_op jit(solution)/shard_map/ppermute | solution.py:31
  101.3 1.3 collective-permute-start.26
  102.6 0.8 copy-done.10
  103.4 1.2 copy-done.15
  104.6 3.0 choose.4.refs_7_.own
  107.6 2.6 collective-permute-start.30
  110.2 6.7 %select_scaled.1 = (bf16[224,2560]{1,0:T(8,128)(2,1)}, bf16[224,2560]{1,0:T(8,128)(2,1)}, bf16[224,2560]{1,0:T(8,128)(2,1)}, bf16[224,2560]{1,0:T(8,128)(2,1)}) custom-call(f32[16,512]{1,0:T(8,128)} %get-tuple-element.68.refs_0_.refs_1_.slots, f32[16,512]{1,0:T(8,128)} %get-tuple-element.69.refs_1_.weights, bf16[128,2560]{1,0:T(8,128)(2,1)} %hold.5.refs_2_, ...), custom_call_target="tpu_custom_call" | custom-call | flops 1 | bytes 1 | tf_op jit(solution)/shard_map/select_scaled/pallas_call | solution.py:249
  116.9 2.3 collective-permute-start.27
  119.2 2.7 collective-permute-start.28
  121.9 1.4 collective-permute-start.29
  124.0 13.2 %hidden.1 = bf16[896,768]{1,0:T(8,128)(2,1)} custom-call(s32[4]{0:T(128)} %pad_add_fusion.2.refs_0_.where, bf16[8,112,2560]{2,1,0:T(8,128)(2,1)} %all-to-all-done.refs_6_.refs_1_, bf16[2560,768]{1,0:T(8,128)(2,1)} %bitcast.22, bf16[2560,768]{1,0:T(8,128)(2,1)} %bitcast.23, bf16[224,2560]{1,0:T(8,128)(2,1)} %get-tuple-element.70.refs_4_), custom_call_target="tpu_custom_call" | custom-call | tf_op jit(solution)/shard_map/hidden/pallas_call | solution.py:303
  137.3 8.5 %down.1.refs_0_ = bf16[8,112,2560]{2,1,0:T(8,128)(2,1)} custom-call(bf16[896,768]{1,0:T(8,128)(2,1)} %hidden.1, bf16[192,2560]{1,0:T(8,128)(2,1)} %pad_maximum_fusion.d0, bf16[192,2560]{1,0:T(8,128)(2,1)} %collective-permute-done.24.d1, bf16[192,2560]{1,0:T(8,128)(2,1)} %collective-permute-done.25.d2, bf16[192,2560]{1,0:T(8,128)(2,1)} %collective-permute-done.26.d3), custom_call_target="tpu_custom_call" | custom-call | tf_op jit(solution)/shard_map/down/pallas_call | solution.py:328
  145.8 5.2 %all-to-all-start.1 = ((bf16[8,112,2560]{2,1,0:T(8,128)(2,1)}), bf16[8,112,2560]{2,1,0:T(8,128)(2,1)}, u32[]{:S(2)}, u32[]{:S(2)}) async-start(bf16[8,112,2560]{2,1,0:T(8,128)(2,1)} %down.1.refs_0_), calls=%async_computation.1 | async-start | bytes 9175040 | tf_op jit(solution)/shard_map/all_to_all | solution.py:448
  151.0 21.8 %collective-permute-done.30.other = bf16[288,2560]{1,0:T(8,128)(2,1)} collective-permute-done((bf16[288,2560]{1,0:T(8,128)(2,1)}, bf16[288,2560]{1,0:T(8,128)(2,1)}, u32[]{:S(2)}, u32[]{:S(2)}) %collective-permute-start.30) | collective-permute-done | bytes 1474592 | tf_op jit(solution)/shard_map/ppermute | solution.py:31
  172.7 3.0 choose.5.refs_4_
  175.8 1.0 copy-done.2
  177.2 3.8 %hold.7 = bf16[448,2560]{1,0:T(8,128)(2,1)} custom-call(bf16[224,2560]{1,0:T(8,128)(2,1)} %get-tuple-element.71.refs_0_, bf16[224,2560]{1,0:T(8,128)(2,1)} %copy-done.2, bf16[224,2560]{1,0:T(8,128)(2,1)} %copy-done.3, bf16[224,2560]{1,0:T(8,128)(2,1)} %collective-permute-done.29.refs_3_, bf16[288,2560]{1,0:T(8,128)(2,1)} %choose.5.refs_4_), custom_call_target="tpu_custom_call" | custom-call | flops 1 | bytes 1 | tf_op jit(solution)/shard_map/hold/pallas_call | solution.py:88
  181.1 4.8 %collective-permute-done.31.refs_4_ = bf16[448,2560]{1,0:T(8,128)(2,1)} collective-permute-done((bf16[448,2560]{1,0:T(8,128)(2,1)}, bf16[448,2560]{1,0:T(8,128)(2,1)}, u32[]{:S(2)}, u32[]{:S(2)}) %collective-permute-start.31) | collective-permute-done | bytes 2293792 | tf_op jit(solution)/shard_map/ppermute | solution.py:31
  185.9 8.8 %grad.1 = (bf16[192,2560]{1,0:T(8,128)(2,1)}, bf16[192,2560]{1,0:T(8,128)(2,1)}, bf16[192,2560]{1,0:T(8,128)(2,1)}, bf16[192,2560]{1,0:T(8,128)(2,1)}) custom-call(s32[4]{0:T(128)} %pad_add_fusion.2.refs_0_.where, bf16[896,768]{1,0:T(8,128)(2,1)} %hidden.1, bf16[224,2560]{1,0:T(8,128)(2,1)} %get-tuple-element.71.refs_0_, bf16[224,2560]{1,0:T(8,128)(2,1)} %copy-done.2, ...), custom_call_target="tpu_custom_call" | custom-call | tf_op jit(solution)/shard_map/grad/pallas_call | solution.py:366
  194.6 1.0 collective-permute-start.32
  195.6 9.3 %collective-permute-start.39 = (bf16[288,2560]{1,0:T(8,128)(2,1)S(1)}, bf16[288,2560]{1,0:T(8,128)(2,1)}, u32[]{:S(2)}, u32[]{:S(2)}) collective-permute-start(bf16[288,2560]{1,0:T(8,128)(2,1)S(1)} %copy-done), channel_id=1, source_target_pairs={{0,2},{1,3},{8,10},{9,11},{16,18},{17,19},{24,26},{25,27},{2,0},{3... | collective-permute-start | bytes 4423688 | tf_op jit(solution)/shard_map/ppermute | solution.py:31
  204.9 1.6 collective-permute-start.37
  206.5 14.0 %all-to-all-done.1.rows = bf16[8,112,2560]{2,1,0:T(8,128)(2,1)} async-done(((bf16[8,112,2560]{2,1,0:T(8,128)(2,1)}), bf16[8,112,2560]{2,1,0:T(8,128)(2,1)}, u32[]{:S(2)}, u32[]{:S(2)}) %all-to-all-start.1) | async-done | bytes 4587552 | tf_op jit(solution)/shard_map/all_to_all | solution.py:448
  220.5 1.0 copy-done.4
  221.5 9.0 %combine.1 = (f32[128,2560]{1,0:T(8,128)}, bf16[128,2560]{1,0:T(8,128)(2,1)}, bf16[128,2560]{1,0:T(8,128)(2,1)}, bf16[128,2560]{1,0:T(8,128)(2,1)}) custom-call(f32[16,512]{1,0:T(8,128)} %get-tuple-element.68.refs_0_.refs_1_.slots, f32[16,512]{1,0:T(8,128)} %get-tuple-element.69.refs_1_.weights, bf16[8,112,2560]{2,1,0:T(8,128)(2,1)} %all-to-all-done.1.rows, ...), custom_call_target="tpu_custom_call" | custom-call | tf_op jit(solution)/shard_map/combine/pallas_call | solution.py:416
  230.4 6.9 %collective-permute-start.33 = (bf16[128,2560]{1,0:T(8,128)(2,1)}, bf16[128,2560]{1,0:T(8,128)(2,1)S(1)}, u32[]{:S(2)}, u32[]{:S(2)}) collective-permute-start(bf16[128,2560]{1,0:T(8,128)(2,1)} %get-tuple-element.76), channel_id=1, source_target_pairs={{0,38},{1,3},{8,46},{9,11},{16,54},{17,19},{24,62},{25,27},{2,0},{... | collective-permute-start | bytes 1966088 | tf_op jit(solution)/shard_map/ppermute | solution.py:31
  237.3 2.7 collective-permute-done.36.c
  239.9 8.3 %collective-permute-done.37.d = bf16[192,2560]{1,0:T(8,128)(2,1)} collective-permute-done((bf16[192,2560]{1,0:T(8,128)(2,1)}, bf16[192,2560]{1,0:T(8,128)(2,1)}, u32[]{:S(2)}, u32[]{:S(2)}) %collective-permute-start.37) | collective-permute-done | bytes 983072 | tf_op jit(solution)/shard_map/ppermute | solution.py:31
  248.2 10.8 %collective-permute-done.33.refs_0_ = bf16[128,2560]{1,0:T(8,128)(2,1)S(1)} collective-permute-done((bf16[128,2560]{1,0:T(8,128)(2,1)}, bf16[128,2560]{1,0:T(8,128)(2,1)S(1)}, u32[]{:S(2)}, u32[]{:S(2)}) %collective-permute-start.33) | collective-permute-done | bytes 655392 | tf_op jit(solution)/shard_map/ppermute | solution.py:31
  259.0 0.9 copy-done.12
  259.9 3.5 %sum.1 = bf16[192,2560]{1,0:T(8,128)(2,1)} custom-call(bf16[192,2560]{1,0:T(8,128)(2,1)} %get-tuple-element.79.a, bf16[192,2560]{1,0:T(8,128)(2,1)} %copy-done.4, bf16[192,2560]{1,0:T(8,128)(2,1)} %copy-done.16, bf16[192,2560]{1,0:T(8,128)(2,1)} %collective-permute-done.37.d, bf16[128,2560]{1,0:T(8,128)(2,1)} %copy-done.12), custom_call_target="tpu_custom_call" | custom-call | flops 1 | bytes 1 | tf_op jit(solution)/shard_map/sum/pallas_call | solution.py:157
  263.4 1.6 broadcast_select_fusion
  265.1 2.1 collective-permute-start.35
  267.2 1.0 add_convert_fusion
  268.4 41.7 %conditional.1 = (bf16[96,2560]{1,0:T(8,128)(2,1)S(1)}, bf16[96,2560]{1,0:T(8,128)(2,1)}) conditional(s32[]{:T(128)} %clamp.3, (bf16[96,2560]{1,0:T(8,128)(2,1)S(1)}, bf16[96,2560]{1,0:T(8,128)(2,1)S(1)}) %tuple.40, (bf16[96,2560]{1,0:T(8,128)(2,1)S(1)}, bf16[96,2560]{1,0:T(8,128)(2,1)S(1)}) %slice_select_fusion, ...), branch_computations={%region_1.2_spmd, %region_2.3_spmd, %region_3.4_spmd, %region_4.5_... | conditional | bytes 4915296 | solution.py:551
  268.4 2.1 collective-permute-start.1
  270.5 6.5 %collective-permute-start.2 = (bf16[96,2560]{1,0:T(8,128)(2,1)S(1)}, bf16[96,2560]{1,0:T(8,128)(2,1)}, u32[]{:S(2)}, u32[]{:S(2)}) collective-permute-start(bf16[96,2560]{1,0:T(8,128)(2,1)S(1)} %get-tuple-element.35), channel_id=1, source_target_pairs={{0,34},{1,35},{8,42},{9,43},{16,50},{17,51},{24,58},{25,59},{2,32}... | collective-permute-start | bytes 1474568 | tf_op jit(solution)/shard_map/cond/branch_1_fun/ppermute | solution.py:31
  277.0 24.4 %collective-permute-done.1 = bf16[96,2560]{1,0:T(8,128)(2,1)S(1)} collective-permute-done((bf16[96,2560]{1,0:T(8,128)(2,1)S(1)}, bf16[96,2560]{1,0:T(8,128)(2,1)S(1)}, u32[]{:S(2)}, u32[]{:S(2)}) %collective-permute-start.1) | collective-permute-done | bytes 491552 | tf_op jit(solution)/shard_map/cond/branch_1_fun/ppermute | solution.py:31
  301.4 8.6 %collective-permute-done.2 = bf16[96,2560]{1,0:T(8,128)(2,1)} collective-permute-done((bf16[96,2560]{1,0:T(8,128)(2,1)S(1)}, bf16[96,2560]{1,0:T(8,128)(2,1)}, u32[]{:S(2)}, u32[]{:S(2)}) %collective-permute-start.2) | collective-permute-done | bytes 491552 | tf_op jit(solution)/shard_map/cond/branch_1_fun/ppermute | solution.py:31
  310.0 2.8 fusion.4
  312.8 0.9 copy-done.17
  313.7 2.7 total.1
  (73 shorter events, 3.5 us)
Async XLA Ops:
  0.6 4.1 %copy-start.20 = (s32[128,6]{0,1:T(8,128)S(1)}, s32[128,6]{0,1:T(8,128)}, u32[]{:S(2)}) copy-start(s32[128,6]{0,1:T(8,128)} %param.20) | copy-start | bytes 9220
  0.6 4.2 %copy-start.19 = (f32[128,6]{0,1:T(8,128)S(1)}, f32[128,6]{0,1:T(8,128)}, u32[]{:S(2)}) copy-start(f32[128,6]{0,1:T(8,128)} %param.21) | copy-start | bytes 9220
  3.2 23.7 %copy-start.21 = (s32[32]{0:T(128)S(1)}, s32[32]{0:T(128)}, u32[]{:S(2)}) copy-start(s32[32]{0:T(128)} %param.22) | copy-start | bytes 388
  3.2 34.3 %collective-permute-start.18 = (bf16[288,2560]{1,0:T(8,128)(2,1)}, bf16[288,2560]{1,0:T(8,128)(2,1)S(1)}, u32[]{:S(2)}, u32[]{:S(2)}) collective-permute-start(bf16[288,2560]{1,0:T(8,128)(2,1)} %hold.4.own), channel_id=1, source_target_pairs={{0,8},{1,9},{8,0},{9,1},{16,24},{17,25},{24,16},{25,17},{2,10},{3,... | collective-permute-start | bytes 4423688 | tf_op jit(solution)/shard_map/ppermute | solution.py:31
  7.7 16.6 %collective-permute-start.15 = (bf16[128,2688]{1,0:T(8,128)(2,1)}, bf16[128,2688]{1,0:T(8,128)(2,1)S(1)}, u32[]{:S(2)}, u32[]{:S(2)}) collective-permute-start(bf16[128,2688]{1,0:T(8,128)(2,1)} %mark.1.refs_1_.refs_2_), channel_id=1, source_target_pairs={{0,2},{1,39},{8,10},{9,47},{16,18},{17,55},{24,26},{25,63},{2,4},{... | collective-permute-start | bytes 2064392 | tf_op jit(solution)/shard_map/ppermute | solution.py:31
  9.7 17.4 %collective-permute-start.16 = (bf16[128,2688]{1,0:T(8,128)(2,1)}, bf16[128,2688]{1,0:T(8,128)(2,1)S(1)}, u32[]{:S(2)}, u32[]{:S(2)}) collective-permute-start(bf16[128,2688]{1,0:T(8,128)(2,1)} %mark.1.refs_1_.refs_2_), channel_id=1, source_target_pairs={{0,38},{1,3},{8,46},{9,11},{16,54},{17,19},{24,62},{25,27},{2,0},{... | collective-permute-start | bytes 2064392 | tf_op jit(solution)/shard_map/ppermute | solution.py:31
  24.4 13.9 %copy-start.6 = (bf16[128,2688]{1,0:T(8,128)(2,1)}, bf16[128,2688]{1,0:T(8,128)(2,1)S(1)}, u32[]{:S(2)}) copy-start(bf16[128,2688]{1,0:T(8,128)(2,1)S(1)} %collective-permute-done.15.refs_2_.refs_3_) | copy-start | bytes 2064388
  24.4 13.1 %collective-permute-start.17 = (bf16[128,2688]{1,0:T(8,128)(2,1)S(1)}, bf16[128,2688]{1,0:T(8,128)(2,1)S(1)}, u32[]{:S(2)}, u32[]{:S(2)}) collective-permute-start(bf16[128,2688]{1,0:T(8,128)(2,1)S(1)} %collective-permute-done.15.refs_2_.refs_3_), channel_id=1, source_target_pairs={{0,2},{1,39},{8,10},{9,47},{16,18},{17,55},{24,26},{25,63},{2,4},{... | collective-permute-start | bytes 2064392 | tf_op jit(solution)/shard_map/ppermute | solution.py:31
  27.1 11.2 %copy-start.7 = (bf16[128,2688]{1,0:T(8,128)(2,1)}, bf16[128,2688]{1,0:T(8,128)(2,1)S(1)}, u32[]{:S(2)}) copy-start(bf16[128,2688]{1,0:T(8,128)(2,1)S(1)} %collective-permute-done.16.refs_3_.refs_4_) | copy-start | bytes 2064388
  37.5 0.9 copy-start.8
  37.5 1.4 copy-start.1
  47.7 62.5 %all-to-all-start = ((bf16[8,112,2560]{2,1,0:T(8,128)(2,1)}), bf16[8,112,2560]{2,1,0:T(8,128)(2,1)}, u32[]{:S(2)}, u32[]{:S(2)}) async-start(bf16[8,112,2560]{2,1,0:T(8,128)(2,1)} %select.94.refs_0_), calls=%async_computation | async-start | bytes 9175040 | tf_op jit(solution)/shard_map/all_to_all | solution.py:448
  54.3 16.8 %collective-permute-start.19 = (bf16[128,2560]{1,0:T(8,128)(2,1)}, bf16[128,2560]{1,0:T(8,128)(2,1)}, u32[]{:S(2)}, u32[]{:S(2)}) collective-permute-start(bf16[128,2560]{1,0:T(8,128)(2,1)} %hold.5.refs_2_), channel_id=1, source_target_pairs={{0,2},{1,39},{8,10},{9,47},{16,18},{17,55},{24,26},{25,63},{2,4},{... | collective-permute-start | bytes 1966088 | tf_op jit(solution)/shard_map/ppermute | solution.py:31
  57.8 29.0 %collective-permute-start.23 = (bf16[96,2560]{1,0:T(8,128)(2,1)}, bf16[96,2560]{1,0:T(8,128)(2,1)}, u32[]{:S(2)}, u32[]{:S(2)}) collective-permute-start(bf16[96,2560]{1,0:T(8,128)(2,1)} %hold.6), channel_id=1, source_target_pairs={{0,32},{1,33},{8,40},{9,41},{16,48},{17,49},{24,56},{25,57},{2,34}... | collective-permute-start | bytes 1474568 | tf_op jit(solution)/shard_map/ppermute | solution.py:31
  63.8 3.9 %copy-start.11 = (bf16[128,2560]{1,0:T(8,128)(2,1)S(1)}, bf16[128,2560]{1,0:T(8,128)(2,1)}, u32[]{:S(2)}) copy-start(bf16[128,2560]{1,0:T(8,128)(2,1)} %hold.5.refs_2_) | copy-start | bytes 1966084
  63.9 22.9 %copy-start.14 = (bf16[96,2560]{1,0:T(8,128)(2,1)S(1)}, bf16[96,2560]{1,0:T(8,128)(2,1)}, u32[]{:S(2)}) copy-start(bf16[96,2560]{1,0:T(8,128)(2,1)} %hold.6) | copy-start | bytes 1474564
  67.0 35.6 %collective-permute-start.22 = (bf16[288,2560]{1,0:T(8,128)(2,1)}, bf16[288,2560]{1,0:T(8,128)(2,1)S(1)}, u32[]{:S(2)}, u32[]{:S(2)}) collective-permute-start(bf16[288,2560]{1,0:T(8,128)(2,1)} %choose.3.own), channel_id=1, source_target_pairs={{0,1},{1,0},{8,9},{9,8},{16,17},{17,16},{24,25},{25,24},{2,3},{3,2... | collective-permute-start | bytes 4423688 | tf_op jit(solution)/shard_map/ppermute | solution.py:31
  67.8 33.5 %collective-permute-start.20 = (bf16[128,2560]{1,0:T(8,128)(2,1)S(1)}, bf16[128,2560]{1,0:T(8,128)(2,1)S(1)}, u32[]{:S(2)}, u32[]{:S(2)}) collective-permute-start(bf16[128,2560]{1,0:T(8,128)(2,1)S(1)} %copy-done.11), channel_id=1, source_target_pairs={{0,38},{1,3},{8,46},{9,11},{16,54},{17,19},{24,62},{25,27},{2,0},{... | collective-permute-start | bytes 1966088 | tf_op jit(solution)/shard_map/ppermute | solution.py:31
  71.1 31.5 %collective-permute-start.21 = (bf16[128,2560]{1,0:T(8,128)(2,1)}, bf16[128,2560]{1,0:T(8,128)(2,1)S(1)}, u32[]{:S(2)}, u32[]{:S(2)}) collective-permute-start(bf16[128,2560]{1,0:T(8,128)(2,1)} %collective-permute-done.19.refs_3_), channel_id=1, source_target_pairs={{0,2},{1,39},{8,10},{9,47},{16,18},{17,55},{24,26},{25,63},{2,4},{... | collective-permute-start | bytes 1966088 | tf_op jit(solution)/shard_map/ppermute | solution.py:31
  88.8 30.4 %collective-permute-start.24 = (bf16[192,2560]{1,0:T(8,128)(2,1)}, bf16[192,2560]{1,0:T(8,128)(2,1)}, u32[]{:S(2)}, u32[]{:S(2)}) collective-permute-start(bf16[192,2560]{1,0:T(8,128)(2,1)} %pad_maximum_fusion.d0), channel_id=1, source_target_pairs={{0,192},{1,193},{8,200},{9,201},{16,208},{17,209},{24,216},{25,217... | collective-permute-start | bytes 2949128 | tf_op jit(solution)/shard_map/ppermute | solution.py:31
  89.3 32.7 %collective-permute-start.25 = (bf16[192,2560]{1,0:T(8,128)(2,1)}, bf16[192,2560]{1,0:T(8,128)(2,1)}, u32[]{:S(2)}, u32[]{:S(2)}) collective-permute-start(bf16[192,2560]{1,0:T(8,128)(2,1)} %pad_maximum_fusion.d0), channel_id=1, source_target_pairs={{0,128},{1,129},{8,136},{9,137},{16,144},{17,145},{24,152},{25,153... | collective-permute-start | bytes 2949128 | tf_op jit(solution)/shard_map/ppermute | solution.py:31
  101.3 1.3 copy-start.9
  101.3 36.0 %collective-permute-start.26 = (bf16[192,2560]{1,0:T(8,128)(2,1)}, bf16[192,2560]{1,0:T(8,128)(2,1)}, u32[]{:S(2)}, u32[]{:S(2)}) collective-permute-start(bf16[192,2560]{1,0:T(8,128)(2,1)} %pad_maximum_fusion.d0), channel_id=1, source_target_pairs={{0,64},{1,65},{8,72},{9,73},{16,80},{17,81},{24,88},{25,89},{2,66}... | collective-permute-start | bytes 2949128 | tf_op jit(solution)/shard_map/ppermute | solution.py:31
  102.5 0.9 copy-start.10
  103.4 1.2 copy-start.15
  107.6 65.1 %collective-permute-start.30 = (bf16[288,2560]{1,0:T(8,128)(2,1)}, bf16[288,2560]{1,0:T(8,128)(2,1)}, u32[]{:S(2)}, u32[]{:S(2)}) collective-permute-start(bf16[288,2560]{1,0:T(8,128)(2,1)} %choose.4.refs_7_.own), channel_id=1, source_target_pairs={{0,4},{1,5},{8,12},{9,13},{16,20},{17,21},{24,28},{25,29},{2,6},{3... | collective-permute-start | bytes 4423688 | tf_op jit(solution)/shard_map/ppermute | solution.py:31
  116.9 58.9 %collective-permute-start.27 = (bf16[224,2560]{1,0:T(8,128)(2,1)}, bf16[224,2560]{1,0:T(8,128)(2,1)S(1)}, u32[]{:S(2)}, u32[]{:S(2)}) collective-permute-start(bf16[224,2560]{1,0:T(8,128)(2,1)} %get-tuple-element.72), channel_id=1, source_target_pairs={{0,8},{1,9},{8,16},{9,17},{16,24},{17,25},{24,0},{25,1},{2,10},{3,... | collective-permute-start | bytes 3440648 | tf_op jit(solution)/shard_map/ppermute | solution.py:31
  119.2 56.6 %collective-permute-start.28 = (bf16[224,2560]{1,0:T(8,128)(2,1)}, bf16[224,2560]{1,0:T(8,128)(2,1)S(1)}, u32[]{:S(2)}, u32[]{:S(2)}) collective-permute-start(bf16[224,2560]{1,0:T(8,128)(2,1)} %get-tuple-element.73), channel_id=1, source_target_pairs={{0,16},{1,17},{8,24},{9,25},{16,0},{17,1},{24,8},{25,9},{2,18},{3,... | collective-permute-start | bytes 3440648 | tf_op jit(solution)/shard_map/ppermute | solution.py:31
  121.9 53.9 %collective-permute-start.29 = (bf16[224,2560]{1,0:T(8,128)(2,1)}, bf16[224,2560]{1,0:T(8,128)(2,1)}, u32[]{:S(2)}, u32[]{:S(2)}) collective-permute-start(bf16[224,2560]{1,0:T(8,128)(2,1)} %get-tuple-element.70.refs_4_), channel_id=1, source_target_pairs={{0,24},{1,25},{8,0},{9,1},{16,8},{17,9},{24,16},{25,17},{2,26},{3,... | collective-permute-start | bytes 3440648 | tf_op jit(solution)/shard_map/ppermute | solution.py:31
  145.8 74.7 %all-to-all-start.1 = ((bf16[8,112,2560]{2,1,0:T(8,128)(2,1)}), bf16[8,112,2560]{2,1,0:T(8,128)(2,1)}, u32[]{:S(2)}, u32[]{:S(2)}) async-start(bf16[8,112,2560]{2,1,0:T(8,128)(2,1)} %down.1.refs_0_), calls=%async_computation.1 | async-start | bytes 9175040 | tf_op jit(solution)/shard_map/all_to_all | solution.py:448
  175.8 1.0 copy-start.2
  175.8 1.4 copy-start.3
  181.1 14.6 %copy-start = (bf16[288,2560]{1,0:T(8,128)(2,1)S(1)}, bf16[288,2560]{1,0:T(8,128)(2,1)}, u32[]{:S(2)}) copy-start(bf16[288,2560]{1,0:T(8,128)(2,1)} %choose.5.refs_4_) | copy-start | bytes 4423684
  181.1 4.8 %collective-permute-start.31 = (bf16[448,2560]{1,0:T(8,128)(2,1)}, bf16[448,2560]{1,0:T(8,128)(2,1)}, u32[]{:S(2)}, u32[]{:S(2)}) collective-permute-start(bf16[448,2560]{1,0:T(8,128)(2,1)} %hold.7), channel_id=1, source_target_pairs={{0,1},{1,0},{8,9},{9,8},{16,17},{17,16},{24,25},{25,24},{2,3},{3,2... | collective-permute-start | bytes 6881288 | tf_op jit(solution)/shard_map/ppermute | solution.py:31
  194.6 25.9 %collective-permute-start.32 = (bf16[192,2560]{1,0:T(8,128)(2,1)}, bf16[192,2560]{1,0:T(8,128)(2,1)S(1)}, u32[]{:S(2)}, u32[]{:S(2)}) collective-permute-start(bf16[192,2560]{1,0:T(8,128)(2,1)} %get-tuple-element.74), channel_id=1, source_target_pairs={{0,64},{1,65},{8,72},{9,73},{16,80},{17,81},{24,88},{25,89},{2,66}... | collective-permute-start | bytes 2949128 | tf_op jit(solution)/shard_map/ppermute | solution.py:31
  195.6 67.8 %collective-permute-start.39 = (bf16[288,2560]{1,0:T(8,128)(2,1)S(1)}, bf16[288,2560]{1,0:T(8,128)(2,1)}, u32[]{:S(2)}, u32[]{:S(2)}) collective-permute-start(bf16[288,2560]{1,0:T(8,128)(2,1)S(1)} %copy-done), channel_id=1, source_target_pairs={{0,2},{1,3},{8,10},{9,11},{16,18},{17,19},{24,26},{25,27},{2,0},{3... | collective-permute-start | bytes 4423688 | tf_op jit(solution)/shard_map/ppermute | solution.py:31
  204.9 35.0 %collective-permute-start.36 = (bf16[192,2560]{1,0:T(8,128)(2,1)}, bf16[192,2560]{1,0:T(8,128)(2,1)S(1)}, u32[]{:S(2)}, u32[]{:S(2)}) collective-permute-start(bf16[192,2560]{1,0:T(8,128)(2,1)} %get-tuple-element.80), channel_id=1, source_target_pairs={{0,128},{1,129},{8,136},{9,137},{16,144},{17,145},{24,152},{25,153... | collective-permute-start | bytes 2949128 | tf_op jit(solution)/shard_map/ppermute | solution.py:31
  204.9 43.3 %collective-permute-start.37 = (bf16[192,2560]{1,0:T(8,128)(2,1)}, bf16[192,2560]{1,0:T(8,128)(2,1)}, u32[]{:S(2)}, u32[]{:S(2)}) collective-permute-start(bf16[192,2560]{1,0:T(8,128)(2,1)} %get-tuple-element.81), channel_id=1, source_target_pairs={{0,192},{1,193},{8,200},{9,201},{16,208},{17,209},{24,216},{25,217... | collective-permute-start | bytes 2949128 | tf_op jit(solution)/shard_map/ppermute | solution.py:31
  220.5 1.0 copy-start.4
  230.4 28.5 %collective-permute-start.33 = (bf16[128,2560]{1,0:T(8,128)(2,1)}, bf16[128,2560]{1,0:T(8,128)(2,1)S(1)}, u32[]{:S(2)}, u32[]{:S(2)}) collective-permute-start(bf16[128,2560]{1,0:T(8,128)(2,1)} %get-tuple-element.76), channel_id=1, source_target_pairs={{0,38},{1,3},{8,46},{9,11},{16,54},{17,19},{24,62},{25,27},{2,0},{... | collective-permute-start | bytes 1966088 | tf_op jit(solution)/shard_map/ppermute | solution.py:31
  239.9 19.0 %copy-start.16 = (bf16[192,2560]{1,0:T(8,128)(2,1)}, bf16[192,2560]{1,0:T(8,128)(2,1)S(1)}, u32[]{:S(2)}) copy-start(bf16[192,2560]{1,0:T(8,128)(2,1)S(1)} %collective-permute-done.36.c) | copy-start | bytes 2949124
  259.0 0.9 copy-start.12
  263.4 4.8 %collective-permute-start.38 = (bf16[192,2560]{1,0:T(8,128)(2,1)}, bf16[192,2560]{1,0:T(8,128)(2,1)S(1)}, u32[]{:S(2)}, u32[]{:S(2)}) collective-permute-start(bf16[192,2560]{1,0:T(8,128)(2,1)} %sum.1), channel_id=1, source_target_pairs={{0,1},{1,0},{8,9},{9,8},{16,17},{17,16},{24,25},{25,24},{2,3},{3,2... | collective-permute-start | bytes 2949128 | tf_op jit(solution)/shard_map/ppermute | solution.py:31
  263.4 3.8 %copy-start.13 = (bf16[128,2560]{1,0:T(8,128)(2,1)S(1)}, bf16[128,2560]{1,0:T(8,128)(2,1)}, u32[]{:S(2)}) copy-start(bf16[128,2560]{1,0:T(8,128)(2,1)} %copy-done.12) | copy-start | bytes 1966084
  263.4 3.8 %copy-start.18 = (bf16[128,2560]{1,0:T(8,128)(2,1)S(1)}, bf16[128,2560]{1,0:T(8,128)(2,1)}, u32[]{:S(2)}) copy-start(bf16[128,2560]{1,0:T(8,128)(2,1)} %get-tuple-element.77) | copy-start | bytes 1966084
  265.1 3.1 copy-start.5
  265.1 47.8 %collective-permute-start.35 = (bf16[128,2560]{1,0:T(8,128)(2,1)}, bf16[128,2560]{1,0:T(8,128)(2,1)S(1)}, u32[]{:S(2)}, u32[]{:S(2)}) collective-permute-start(bf16[128,2560]{1,0:T(8,128)(2,1)} %get-tuple-element.78), channel_id=1, source_target_pairs={{0,2},{1,39},{8,10},{9,47},{16,18},{17,55},{24,26},{25,63},{2,4},{... | collective-permute-start | bytes 1966088 | tf_op jit(solution)/shard_map/ppermute | solution.py:31
  268.2 44.7 %collective-permute-start.34 = (bf16[128,2560]{1,0:T(8,128)(2,1)}, bf16[128,2560]{1,0:T(8,128)(2,1)}, u32[]{:S(2)}, u32[]{:S(2)}) collective-permute-start(bf16[128,2560]{1,0:T(8,128)(2,1)} %add_convert_fusion), channel_id=1, source_target_pairs={{0,38},{1,3},{8,46},{9,11},{16,54},{17,19},{24,62},{25,27},{2,0},{... | collective-permute-start | bytes 1966088 | tf_op jit(solution)/shard_map/ppermute | solution.py:31
  268.4 33.0 %collective-permute-start.1 = (bf16[96,2560]{1,0:T(8,128)(2,1)S(1)}, bf16[96,2560]{1,0:T(8,128)(2,1)S(1)}, u32[]{:S(2)}, u32[]{:S(2)}) collective-permute-start(bf16[96,2560]{1,0:T(8,128)(2,1)S(1)} %get-tuple-element.34), channel_id=1, source_target_pairs={{0,2},{1,3},{8,10},{9,11},{16,18},{17,19},{24,26},{25,27},{2,0},{3... | collective-permute-start | bytes 1474568 | tf_op jit(solution)/shard_map/cond/branch_1_fun/ppermute | solution.py:31
  270.5 39.5 %collective-permute-start.2 = (bf16[96,2560]{1,0:T(8,128)(2,1)S(1)}, bf16[96,2560]{1,0:T(8,128)(2,1)}, u32[]{:S(2)}, u32[]{:S(2)}) collective-permute-start(bf16[96,2560]{1,0:T(8,128)(2,1)S(1)} %get-tuple-element.35), channel_id=1, source_target_pairs={{0,34},{1,35},{8,42},{9,43},{16,50},{17,51},{24,58},{25,59},{2,32}... | collective-permute-start | bytes 1474568 | tf_op jit(solution)/shard_map/cond/branch_1_fun/ppermute | solution.py:31
  312.8 0.9 copy-start.17
